TPU v7x, 32 devices: a whole 2x2x4 slice. The times are simulated.
32 devices in a mesh: req: 4 (over y, core), vocab: 8 (over z, x).
Axes of the slice: x: 2, y: 2, z: 4, core: 2. Of those that a mesh axis runs over, the one named last changes fastest.
Arguments:
- hidden_rows: bfloat16 [1024, 2048], P(('req', 'vocab')), may hold values from -20 to 20
- norm_gain: float32 [2048], replicated, may hold values from 0.1 to 1.9
- head_weight: bfloat16 [2048, 81920], P(None, 'vocab'), may hold values from -10 to 10
- token_ids: int32 [1024], P('req'), may hold values from 0 to 81919
- live_count: int32 [32], P(('req', 'vocab')), may hold values from 1 to 32, as said below
Outputs:
- logprob: float32 [1024], P(('req', 'vocab'))
- entropy: float32 [1024], P(('req', 'vocab'))
Inputs may be any that keep to these rules, and one draw needn't show every extreme that they name: `live_count`: the live rows of an owner are its first ones; some owner has all 32 live in every draw.
All inputs are finite; a program needn't handle non-finite values.
Results may differ from a plain program's by a relative error of at most 0.012.
Values may be sent and summed in bfloat16 or wider, within the bound.
No kernel may reach another device: no remote copies, remote signals or barrier semaphores. Data moves between devices by JAX's collectives and lax.ppermute only.
A program may use at most 128 MiB of HBM per device.

v0:
```python
import jax
import jax.numpy as jnp
from jax import lax
from jax.sharding import PartitionSpec as P


def local_stats(row_block, labels, columns, first_col):
    logits = jnp.dot(row_block, columns, preferred_element_type=jnp.float32)
    row_top = jnp.max(logits, axis=1)
    shifted = logits - row_top[:, None]
    powers = jnp.exp(shifted)
    row_total = jnp.sum(powers, axis=1)
    row_spread = jnp.sum(powers * shifted, axis=1)
    width = columns.shape[1]
    offset = labels - first_col
    inside = (offset >= 0) & (offset < width)
    chosen = jnp.take_along_axis(logits, jnp.clip(offset, 0, width - 1)[:, None], axis=1)[:, 0]
    row_picked = jnp.where(inside, chosen, 0.0)
    return (row_top, row_total, row_spread, row_picked)


def rescale(row_top, row_total, row_spread, global_top):
    factor = jnp.exp(row_top - global_top)
    return (row_total * factor, (row_spread + (row_top - global_top) * row_total) * factor)


def finish(global_top, row_total, row_spread, row_picked, live_count, own_rows):
    log_total = jnp.log(row_total)
    logprob = row_picked - global_top - log_total
    entropy = log_total - row_spread / row_total
    live = jnp.arange(own_rows, dtype=jnp.int32) < live_count[0]
    return (jnp.where(live, logprob, 0.0), jnp.where(live, entropy, 0.0))


def own_slice(array, start, own_rows):
    return lax.dynamic_slice_in_dim(array, start, own_rows, 0)


def per_device(hidden_rows, norm_gain, head_weight, token_ids, live_count):
    own_rows = hidden_rows.shape[0]
    shard_width = head_weight.shape[1]
    values = hidden_rows.astype(jnp.float32)
    squares = jnp.mean(values * values, axis=1)
    normed = (values * lax.rsqrt(squares + 1e-06)[:, None] * norm_gain[None, :]).astype(
        jnp.bfloat16
    )
    gathered = lax.all_gather(normed, "vocab", axis=0, tiled=True)
    first_col = lax.axis_index("vocab") * shard_width
    row_top, row_total, row_spread, row_picked = local_stats(
        gathered, token_ids, head_weight, first_col
    )
    start = lax.axis_index("vocab") * own_rows
    global_top = lax.pmax(row_top, "vocab")
    scaled_total, scaled_spread = rescale(row_top, row_total, row_spread, global_top)
    summed_total, summed_spread, summed_picked = lax.psum(
        (scaled_total, scaled_spread, row_picked), "vocab"
    )
    return finish(
        own_slice(global_top, start, own_rows),
        own_slice(summed_total, start, own_rows),
        own_slice(summed_spread, start, own_rows),
        own_slice(summed_picked, start, own_rows),
        live_count,
        own_rows,
    )


def solution(mesh):
    placed = (P(("req", "vocab"), None), P(), P(None, "vocab"), P("req"), P(("req", "vocab")))
    return jax.shard_map(
        per_device,
        mesh=mesh,
        in_specs=placed,
        out_specs=(P(("req", "vocab")), P(("req", "vocab"))),
        check_vma=False,
    )
```

profile of v0, /device:TPU:0, one launch (start us, length us, event | category | flops | bytes accessed | tf_op | source)
XLA Modules:
  0.0 128.7 jit_solution(6078410618957968155)
XLA Ops:
  7.2 0.0 all-gather.2.cloned.1.call-start
  7.2 1.0 fusion.1
  8.3 1.7 %fusion.3 = bf16[32,2048]{1,0:T(8,128)(2,1)} fusion(bf16[32,2048]{1,0:T(8,128)(2,1)} %param.5, f32[2048]{0:T(1024)} %param.6, f32[32]{0:T(128)S(1)} %add_rsqrt_fusion), kind=kLoop, calls=%fused_computation.8 | loop fusion | flops 262144 | bytes 270464 | tf_op jit(solution)/shard_map/convert_element_type | solution.py:44
  9.9 0.0 all-gather.2.cloned.1.call-update
  10.6 0.7 compare_select_fusion
  11.3 41.7 %all-gather.2.cloned.1.call-done = bf16[256,2048]{1,0:T(8,128)(2,1)} async-done(((bf16[32,2048]{1,0:T(8,128)(2,1)}), bf16[256,2048]{1,0:T(8,128)(2,1)}) %all-gather.2.cloned.1.call-update) | async-done | bytes 1048592 | tf_op jit(solution)/shard_map/all_gather | solution.py:47
  53.0 21.1 %fusion.7 = (f32[256]{0:T(256)S(1)}, f32[256,10240]{1,0:T(8,128)}) fusion(bf16[256,2048]{1,0:T(8,128)(2,1)} %all-gather.2.cloned.1.call-done, bf16[2048,10240]{1,0:T(8,128)(2,1)} %param.7), kind=kOutput, calls=%fused_computation.23 | convolution fusion | flops 10740039680 | bytes 53478400 | tf_op jit(solution)/shard_map/dot_general | solution.py:8
  74.1 0.0 copy-start
  74.1 19.3 %pmax.7 = f32[256]{0:T(256)S(1)} all-reduce(f32[256]{0:T(256)S(1)} %get-tuple-element.11), channel_id=1, replica_groups=mesh['req'=4,'vocab'=8] {'vocab'}, use_global_device_ids=true, to_apply=%region_3.0 | all-reduce | flops 256 | bytes 2048 | tf_op jit(solution)/shard_map/pmax | solution.py:53
  93.5 6.3 %fusion = (f32[256]{0:T(256)S(1)}, f32[256]{0:T(256)S(1)}) fusion(f32[256,10240]{1,0:T(8,128)} %get-tuple-element.12, f32[256]{0:T(256)S(1)} %get-tuple-element.11), kind=kLoop, calls=%fused_computation.3 | loop fusion | flops 10485248 | bytes 10488832 | tf_op jit(solution)/shard_map/reduce_sum | solution.py:13
  99.7 4.3 %gather_fusion = f32[256]{0:T(256)S(1)} fusion(f32[256,10240]{1,0:T(8,128)} %get-tuple-element.12, s32[256]{0:T(256)S(1)} %bitcast.8), kind=kCustom, calls=%fused_computation | custom fusion | bytes 4096 | tf_op jit(solution)/shard_map/jit(take_along_axis)/gather | solution.py:17
  104.1 0.0 copy-done
  104.1 17.1 %all-reduce = (f32[256]{0:T(256)S(1)}, f32[256]{0:T(256)S(1)}, f32[256]{0:T(256)S(1)}) all-reduce(f32[256]{0:T(256)S(1)} %and_select_fusion.1, f32[256]{0:T(256)S(1)} %get-tuple-element.8, f32[256]{0:T(256)S(1)} %get-tuple-element.7), channel_id=1, replica_groups=mesh['req'=4,'vocab'=8] {'vocab'}, use_global_device_ids=true, to_apply=%region_1.0 | all-reduce | flops 768 | bytes 6144 | tf_op jit(solution)/shard_map/psum | solution.py:55
  121.2 0.6 compare_select_fusion.1
  (6 shorter events, 0.1 us)
Async XLA Ops:
  7.2 45.8 %all-gather.2.cloned.1.call-start = ((), (), s32[]{:S(2)}) async-start(), calls=%async_computation | async-start | bytes 1179648 | tf_op jit(solution)/shard_map/all_gather | solution.py:47
  74.1 29.9 %copy-start = (s32[256]{0:T(256)S(1)}, s32[256]{0:T(256)}, u32[]{:S(2)}) copy-start(s32[256]{0:T(256)} %param.8) | copy-start | bytes 3076
Sparse Core Ops, SparseCore 0:
  10.1 42.8 all-gather.1
where the time goes:
time: 129 us
  waiting for transfers between devices  41.7 us (32%)
  blocking collectives  36.4 us (28%)
  matrix products  21.1 us (16%)
  between operations  14.7 us (11%)
  other arithmetic  10.3 us (8%)
  local copies, waits for them, and re-layouts  4.31 us (3%)
    all_gather x1, waiting for transfers between devices, per_device(): gathered = lax.all_gather(normed, 'vocab', axis=0, tiled=True)  41.7 us
    dot_general x1, matrix products, local_stats(): logits = jnp.dot(row_block, columns, preferred_element_type=jnp.float32)  21.1 us
    pmax x1, blocking collectives, per_device(): global_top = lax.pmax(row_top, 'vocab')  19.3 us
    psum x1, blocking collectives, per_device(): lax.psum((scaled_total, scaled_spread, row_picked), 'vocab')  17.1 us
    reduce_sum x1, other arithmetic, local_stats(): row_spread = jnp.sum(powers * shifted, axis=1)  6.29 us
    gather x1, local copies, waits for them, and re-layouts, local_stats(): jnp.take_along_axis(logits, jnp.clip(offset, 0, width - 1)[:, None], axis=1)  4.3 us
  transfers between devices with their start and end apart: 1, of which 1 were waited for; matrix products, arithmetic and copies ran while one was open for 1% of the time, Pallas kernels for 0%

commit v1 on v0

v1 whole, which is shorter than its diff:
```python
import functools

import jax
import jax.numpy as jnp
from jax import lax
from jax.experimental import pallas as pl
from jax.experimental.pallas import tpu as pltpu
from jax.sharding import PartitionSpec as P

LANES = 128
LOWEST = -1e30
VMEM = pl.BlockSpec(memory_space=pltpu.VMEM)


def norm_kernel(hidden_ref, gain_ref, out_ref):
    values = hidden_ref[...].astype(jnp.float32)
    squares = jnp.mean(values * values, axis=1, keepdims=True)
    out_ref[...] = (values * lax.rsqrt(squares + 1e-06) * gain_ref[...]).astype(jnp.bfloat16)


def normalise(hidden_rows, norm_gain):
    return pl.pallas_call(
        norm_kernel,
        in_specs=[VMEM, VMEM],
        out_specs=VMEM,
        out_shape=jax.ShapeDtypeStruct(hidden_rows.shape, jnp.bfloat16),
    )(hidden_rows, norm_gain[None, :])


def head_kernel(n_blocks, tile, *refs):
    block_refs = refs[:n_blocks]
    token_ref, head_ref, out_ref, rows, logits, wanted, top, total, spread, picked = refs[n_blocks:]
    own_rows = block_refs[0].shape[0]
    width = head_ref.shape[1]
    n_rows = rows.shape[0]
    n_tiles = width // tile
    me = lax.axis_index("vocab")
    for distance, block in enumerate(block_refs):
        start = pl.multiple_of(lax.bitwise_xor(me, distance) * own_rows, own_rows)
        rows[pl.ds(start, own_rows), :] = block[...]

    lane = lax.broadcasted_iota(jnp.int32, (n_rows, LANES), 1)
    wanted[...] = token_ref[...] - me * width - lane
    top[...] = jnp.full(top.shape, LOWEST, jnp.float32)
    total[...] = jnp.zeros(total.shape, jnp.float32)
    spread[...] = jnp.zeros(spread.shape, jnp.float32)
    picked[...] = jnp.zeros(picked.shape, jnp.float32)

    def multiply(index, slot):
        columns = pl.ds(pl.multiple_of(index * tile, tile), tile)
        logits[slot] = jnp.dot(rows[...], head_ref[:, columns], preferred_element_type=jnp.float32)

    def gather_stats(index, slot):
        step = 32
        for first in range(0, n_rows, step):
            part = slice(first, first + step)
            pieces = [logits[slot, part, c : c + LANES] for c in range(0, tile, LANES)]
            old = top[part]
            new = jnp.maximum(old, functools.reduce(jnp.maximum, pieces))
            shift = old - new
            factor = jnp.exp(shift)
            sums = total[part]
            spreads = (spread[part] + shift * sums) * factor
            sums = sums * factor
            found = picked[part]
            target = wanted[part]
            for number, piece in enumerate(pieces):
                shifted = piece - new
                power = jnp.exp(shifted)
                sums = sums + power
                spreads = spreads + power * shifted
                found = jnp.where(target == index * tile + number * LANES, piece, found)
            top[part] = new
            total[part] = sums
            spread[part] = spreads
            picked[part] = found

    multiply(0, 0)

    @pl.loop(0, n_tiles // 2 - 1)
    def _(pair):
        index = pair * 2
        multiply(index + 1, 1)
        gather_stats(index, 0)
        multiply(index + 2, 0)
        gather_stats(index + 1, 1)

    multiply(n_tiles - 1, 1)
    gather_stats(n_tiles - 2, 0)
    gather_stats(n_tiles - 1, 1)

    row_top = jnp.max(top[...], axis=1, keepdims=True)
    shift = top[...] - row_top
    factor = jnp.exp(shift)
    row_total = jnp.sum(total[...] * factor, axis=1, keepdims=True)
    row_spread = jnp.sum((spread[...] + shift * total[...]) * factor, axis=1, keepdims=True)
    row_picked = jnp.sum(picked[...], axis=1, keepdims=True)
    packed = jnp.where(
        lane == 0,
        row_top,
        jnp.where(lane == 1, row_total, jnp.where(lane == 2, row_spread, row_picked)),
    )
    out_ref[...] = packed.T[:8, :]


def head_stats(blocks, token_ids, head_weight):
    own_rows, depth = blocks[0].shape
    n_rows = own_rows * len(blocks)
    width = head_weight.shape[1]
    tile = next(t for t in (1024, 512, 256, 128) if width % (2 * t) == 0)
    head_weight = pltpu.with_memory_space_constraint(head_weight, pltpu.VMEM)
    return pl.pallas_call(
        functools.partial(head_kernel, len(blocks), tile),
        in_specs=[VMEM] * (len(blocks) + 2),
        out_specs=VMEM,
        out_shape=jax.ShapeDtypeStruct((8, n_rows), jnp.float32),
        scratch_shapes=[
            pltpu.VMEM((n_rows, depth), jnp.bfloat16),
            pltpu.VMEM((2, n_rows, tile), jnp.float32),
            pltpu.VMEM((n_rows, LANES), jnp.int32),
            pltpu.VMEM((n_rows, LANES), jnp.float32),
            pltpu.VMEM((n_rows, LANES), jnp.float32),
            pltpu.VMEM((n_rows, LANES), jnp.float32),
            pltpu.VMEM((n_rows, LANES), jnp.float32),
        ],
        compiler_params=pltpu.CompilerParams(vmem_limit_bytes=18 * 2**20),
        cost_estimate=pl.CostEstimate(
            flops=2 * n_rows * depth * width,
            bytes_accessed=2 * n_rows * depth,
            transcendentals=n_rows * width,
        ),
    )(*blocks, token_ids[:, None], head_weight)


def merge(mine, theirs):
    top = jnp.maximum(mine[0:1], theirs[0:1])
    a, b = mine[0:1] - top, theirs[0:1] - top
    fa, fb = jnp.exp(a), jnp.exp(b)
    total = mine[1:2] * fa + theirs[1:2] * fb
    spread = (mine[2:3] + a * mine[1:2]) * fa + (theirs[2:3] + b * theirs[1:2]) * fb
    return top, total, spread, mine[3:4] + theirs[3:4]


def merge_kernel(mine_ref, theirs_ref, out_ref):
    for row, value in enumerate(merge(mine_ref[...], theirs_ref[...])):
        out_ref[row : row + 1, :] = value
    out_ref[4:8, :] = jnp.zeros((4, out_ref.shape[1]), jnp.float32)


def finish_kernel(own_rows, live_ref, mine_ref, theirs_ref, logprob_ref, entropy_ref):
    top, total, spread, picked = merge(mine_ref[...], theirs_ref[...])
    log_total = jnp.log(total)
    logprob = picked - top - log_total
    entropy = log_total - spread / total
    n_rows = logprob.shape[1]
    start = lax.axis_index("vocab") * own_rows
    logprob = pltpu.roll(logprob, n_rows - start, 1)
    entropy = pltpu.roll(entropy, n_rows - start, 1)
    live = lax.broadcasted_iota(jnp.int32, logprob.shape, 1) < live_ref[0]
    logprob_ref[...] = jnp.where(live, logprob, 0.0)[:, :own_rows]
    entropy_ref[...] = jnp.where(live, entropy, 0.0)[:, :own_rows]


def swap(array, distance, size):
    return lax.ppermute(array, "vocab", [(i, i ^ distance) for i in range(size)])


def per_device(size, hidden_rows, norm_gain, head_weight, token_ids, live_count):
    own_rows = hidden_rows.shape[0]
    normed = normalise(hidden_rows, norm_gain)
    blocks = {0: normed}
    for distance in range(size - 2, 0, -2):
        blocks[distance] = swap(normed, distance, size)
    for distance in range(0, size, 2):
        blocks[distance + 1] = swap(blocks[distance], 1, size)
    stats = head_stats([blocks[d] for d in range(size)], token_ids, head_weight)
    distance = 1
    while 2 * distance < size:
        stats = pl.pallas_call(
            merge_kernel,
            in_specs=[VMEM, VMEM],
            out_specs=VMEM,
            out_shape=jax.ShapeDtypeStruct(stats.shape, jnp.float32),
        )(stats, swap(stats, distance, size))
        distance *= 2
    out = jax.ShapeDtypeStruct((1, own_rows), jnp.float32)
    logprob, entropy = pl.pallas_call(
        functools.partial(finish_kernel, own_rows),
        in_specs=[pl.BlockSpec(memory_space=pltpu.SMEM), VMEM, VMEM],
        out_specs=(VMEM, VMEM),
        out_shape=(out, out),
    )(live_count, stats, swap(stats, distance, size))
    return logprob[0], entropy[0]


def solution(mesh):
    placed = (P(("req", "vocab"), None), P(), P(None, "vocab"), P("req"), P(("req", "vocab")))
    return jax.shard_map(
        functools.partial(per_device, mesh.shape["vocab"]),
        mesh=mesh,
        in_specs=placed,
        out_specs=(P(("req", "vocab")), P(("req", "vocab"))),
        check_vma=False,
    )
```

time: 129 us -> 72.1 us (0.56)
  blocking collectives: 36.4 us -> 0 us
  waiting for transfers between devices: 41.7 us -> 18.3 us
  matrix products: 21.1 us -> 0 us
  Pallas kernels: 0 us -> 20.5 us
  starting transfers between devices: 0.04 us -> 14.6 us
  between operations: 14.7 us -> 1.35 us
  local copies, waits for them, and re-layouts: 4.31 us -> 16.8 us
  other arithmetic: 10.3 us -> 0 us
    all_gather x1 -> x0, waiting for transfers between devices: 41.7 us -> none  [per_device(): gathered = lax.all_gather(normed, 'vocab', axis=0, tiled=True)]
    dot_general x1 -> x0, matrix products: 21.1 us -> none  [local_stats(): logits = jnp.dot(row_block, columns, preferred_element_type=jnp.float32)]
    pallas_call x0 -> x5, Pallas kernels: none -> 20.5 us  [the longest x1 14.8 us: head_stats(): pl.pallas_call(functools.partial(head_kernel, len(blocks), tile), in_spec...]
    pmax x1 -> x0, blocking collectives: 19.3 us -> none  [per_device(): global_top = lax.pmax(row_top, 'vocab')]
    ppermute x0 -> x10, waiting for transfers between devices: none -> 18.3 us  [swap(): lax.ppermute(array, 'vocab', [(i, i ^ distance) for i in range(size)])]
    psum x1 -> x0, blocking collectives: 17.1 us -> none  [per_device(): lax.psum((scaled_total, scaled_spread, row_picked), 'vocab')]
    unnamed x3 -> x22, local copies, waits for them, and re-layouts: 0.01 us -> 15.4 us
    ppermute x0 -> x10, starting transfers between devices: none -> 14.6 us  [swap(): lax.ppermute(array, 'vocab', [(i, i ^ distance) for i in range(size)])]
  transfers between devices with their start and end apart: 1 -> 10, of which waited for: 1 -> 7; matrix products, arithmetic and copies ran while one was open for 1% -> 2% of each run, Pallas kernels for 0% -> 0%
where the time goes in v1:
time: 72.1 us; the launch traced here: 71.6 us
  Pallas kernels  20.5 us (28%)
  waiting for transfers between devices  18.3 us (25%)
  local copies, waits for them, and re-layouts  16.8 us (23%)
  starting transfers between devices  14.6 us (20%)
  between operations  1.35 us (2%)
    ppermute x10, waiting for transfers between devices, swap(): lax.ppermute(array, 'vocab', [(i, i ^ distance) for i in range(size)])  18.3 us
    unnamed x22, local copies, waits for them, and re-layouts  15.4 us
    pallas_call x1, Pallas kernels, head_stats(): pl.pallas_call(functools.partial(head_kernel, len(blocks), tile), in_spec...  14.8 us
    ppermute x10, starting transfers between devices, swap(): lax.ppermute(array, 'vocab', [(i, i ^ distance) for i in range(size)])  14.6 us
    pallas_call x2, Pallas kernels, per_device(): pl.pallas_call(merge_kernel, in_specs=[VMEM, VMEM], out_specs=VMEM, out_s...  2.66 us
    pallas_call x1, Pallas kernels, normalise(): pl.pallas_call(norm_kernel, in_specs=[VMEM, VMEM], out_specs=VMEM, out_sh...  1.68 us
    broadcast_in_dim x1, local copies, waits for them, and re-layouts, head_stats(): token_ids[:, None]  1.47 us
  transfers between devices with their start and end apart: 10, of which 7 were waited for; matrix products, arithmetic and copies ran while one was open for 2% of the time, Pallas kernels for 0%

profile of v1, /device:TPU:0, one launch (start us, length us, event | category | flops | bytes accessed | tf_op | source)
XLA Modules:
  0.0 71.6 jit_solution(16933242824051387486)
XLA Ops:
  0.6 1.7 %shard_map.68.refs_0_ = bf16[32,2048]{1,0:T(8,128)(2,1)} custom-call(bf16[32,2048]{1,0:T(8,128)(2,1)} %hidden_ref.1, f32[1,2048]{1,0:T(1,128)} %bitcast.4), custom_call_target="tpu_custom_call" | custom-call | tf_op jit(solution)/shard_map/pallas_call | solution.py:22
  2.3 3.0 %collective-permute-start.1 = (bf16[32,2048]{1,0:T(8,128)(2,1)}, bf16[32,2048]{1,0:T(8,128)(2,1)S(1)}, u32[]{:S(2)}, u32[]{:S(2)}) collective-permute-start(bf16[32,2048]{1,0:T(8,128)(2,1)} %shard_map.68.refs_0_), channel_id=1, source_target_pairs={{0,2},{1,3},{2,0},{3,1},{4,6},{5,7},{6,4},{7,5},{8,10},{9,11},{10,... | collective-permute-start | bytes 393224 | tf_op jit(solution)/shard_map/ppermute | solution.py:165
  5.3 2.6 %collective-permute-start.3 = (bf16[32,2048]{1,0:T(8,128)(2,1)}, bf16[32,2048]{1,0:T(8,128)(2,1)S(1)}, u32[]{:S(2)}, u32[]{:S(2)}) collective-permute-start(bf16[32,2048]{1,0:T(8,128)(2,1)} %shard_map.68.refs_0_), channel_id=1, source_target_pairs={{0,4},{1,5},{2,6},{3,7},{4,0},{5,1},{6,2},{7,3},{8,12},{9,13},{10,... | collective-permute-start | bytes 393224 | tf_op jit(solution)/shard_map/ppermute | solution.py:165
  7.9 0.0 collective-permute-start.5
  7.9 1.7 %collective-permute-start = (bf16[32,2048]{1,0:T(8,128)(2,1)}, bf16[32,2048]{1,0:T(8,128)(2,1)S(1)}, u32[]{:S(2)}, u32[]{:S(2)}) collective-permute-start(bf16[32,2048]{1,0:T(8,128)(2,1)} %shard_map.68.refs_0_), channel_id=1, source_target_pairs={{0,1},{1,0},{2,3},{3,2},{4,5},{5,4},{6,7},{7,6},{8,9},{9,8},{10,11... | collective-permute-start | bytes 393224 | tf_op jit(solution)/shard_map/ppermute | solution.py:165
  9.6 0.9 %collective-permute-done.1.refs_2_ = bf16[32,2048]{1,0:T(8,128)(2,1)S(1)} collective-permute-done((bf16[32,2048]{1,0:T(8,128)(2,1)}, bf16[32,2048]{1,0:T(8,128)(2,1)S(1)}, u32[]{:S(2)}, u32[]{:S(2)}) %collective-permute-start.1) | collective-permute-done | bytes 131104 | tf_op jit(solution)/shard_map/ppermute | solution.py:165
  10.6 0.0 copy-start.1
  10.6 1.7 %collective-permute-start.2 = (bf16[32,2048]{1,0:T(8,128)(2,1)S(1)}, bf16[32,2048]{1,0:T(8,128)(2,1)S(1)}, u32[]{:S(2)}, u32[]{:S(2)}) collective-permute-start(bf16[32,2048]{1,0:T(8,128)(2,1)S(1)} %collective-permute-done.1.refs_2_), channel_id=1, source_target_pairs={{0,1},{1,0},{2,3},{3,2},{4,5},{5,4},{6,7},{7,6},{8,9},{9,8},{10,11... | collective-permute-start | bytes 393224 | tf_op jit(solution)/shard_map/ppermute | solution.py:165
  12.3 6.2 %collective-permute-done.3.refs_4_ = bf16[32,2048]{1,0:T(8,128)(2,1)S(1)} collective-permute-done((bf16[32,2048]{1,0:T(8,128)(2,1)}, bf16[32,2048]{1,0:T(8,128)(2,1)S(1)}, u32[]{:S(2)}, u32[]{:S(2)}) %collective-permute-start.3) | collective-permute-done | bytes 131104 | tf_op jit(solution)/shard_map/ppermute | solution.py:165
  18.5 0.0 copy-start.2
  18.5 1.5 %collective-permute-start.4 = (bf16[32,2048]{1,0:T(8,128)(2,1)S(1)}, bf16[32,2048]{1,0:T(8,128)(2,1)S(1)}, u32[]{:S(2)}, u32[]{:S(2)}) collective-permute-start(bf16[32,2048]{1,0:T(8,128)(2,1)S(1)} %collective-permute-done.3.refs_4_), channel_id=1, source_target_pairs={{0,1},{1,0},{2,3},{3,2},{4,5},{5,4},{6,7},{7,6},{8,9},{9,8},{10,11... | collective-permute-start | bytes 393224 | tf_op jit(solution)/shard_map/ppermute | solution.py:165
  20.0 0.0 collective-permute-done.5.refs_6_
  20.0 0.0 copy-start.3
  20.0 0.5 collective-permute-start.6
  20.5 1.5 %copy.7.refs_8_ = s32[256,1]{1,0:T(8,128)} copy(s32[256,1]{0,1:T(1,128)} %bitcast.5) | data formatting | bytes 2048 | tf_op jit(solution)/shard_map/broadcast_in_dim | solution.py:132
  22.0 0.0 collective-permute-done.refs_1_
  22.0 0.0 copy-start.4
  22.0 0.0 collective-permute-done.2.refs_3_
  22.0 0.0 copy-start.5
  22.0 1.4 %collective-permute-done.4.refs_5_ = bf16[32,2048]{1,0:T(8,128)(2,1)S(1)} collective-permute-done((bf16[32,2048]{1,0:T(8,128)(2,1)S(1)}, bf16[32,2048]{1,0:T(8,128)(2,1)S(1)}, u32[]{:S(2)}, u32[]{:S(2)}) %collective-permute-start.4) | collective-permute-done | bytes 131104 | tf_op jit(solution)/shard_map/ppermute | solution.py:165
  23.5 0.0 copy-start.6
  23.5 1.5 %collective-permute-done.6.refs_7_ = bf16[32,2048]{1,0:T(8,128)(2,1)S(1)} collective-permute-done((bf16[32,2048]{1,0:T(8,128)(2,1)S(1)}, bf16[32,2048]{1,0:T(8,128)(2,1)S(1)}, u32[]{:S(2)}, u32[]{:S(2)}) %collective-permute-start.6) | collective-permute-done | bytes 131104 | tf_op jit(solution)/shard_map/ppermute | solution.py:165
  25.0 0.0 copy-done.1
  25.0 0.0 copy-done.2
  25.0 0.0 copy-done.3
  25.0 0.0 copy-done.4
  25.0 0.0 copy-done.5
  25.0 0.0 copy-done.6
  25.0 0.0 copy-start.7
  25.0 0.6 copy-done.7
  25.6 0.0 copy-start
  25.6 12.9 %copy-done = bf16[2048,10240]{1,0:T(8,128)(2,1)S(1)} copy-done((bf16[2048,10240]{1,0:T(8,128)(2,1)S(1)}, bf16[2048,10240]{1,0:T(8,128)(2,1)}, u32[]{:S(2)}) %copy-start) | copy-done | bytes 41943064
  38.6 14.8 %shard_map.69.mine_ref = f32[8,256]{1,0:T(8,128)} custom-call(bf16[32,2048]{1,0:T(8,128)(2,1)} %shard_map.68.refs_0_, bf16[32,2048]{1,0:T(8,128)(2,1)} %copy-done.4, bf16[32,2048]{1,0:T(8,128)(2,1)} %copy-done.1, bf16[32,2048]{1,0:T(8,128)(2,1)} %copy-done.5, bf16[32,2048]{1,0:T(8,128)(2,1)} %copy-done.2, bf16[32,2048]{1,0:T(8,128)(2,1)} %copy-done.6, ...), custom_call_target="tpu_custom_call" | custom-call | flops 10737418240 | bytes 1048576 | tf_op jit(solution)/shard_map/pallas_call | solution.py:112
  53.4 1.4 %collective-permute-start.7 = (f32[8,256]{1,0:T(8,128)}, f32[8,256]{1,0:T(8,128)S(1)}, u32[]{:S(2)}, u32[]{:S(2)}) collective-permute-start(f32[8,256]{1,0:T(8,128)} %shard_map.69.mine_ref), channel_id=1, source_target_pairs={{0,1},{1,0},{2,3},{3,2},{4,5},{5,4},{6,7},{7,6},{8,9},{9,8},{10,11... | collective-permute-start | bytes 24584 | tf_op jit(solution)/shard_map/ppermute | solution.py:165
  54.8 2.5 %collective-permute-done.7.theirs_ref = f32[8,256]{1,0:T(8,128)S(1)} collective-permute-done((f32[8,256]{1,0:T(8,128)}, f32[8,256]{1,0:T(8,128)S(1)}, u32[]{:S(2)}, u32[]{:S(2)}) %collective-permute-start.7) | collective-permute-done | bytes 8224 | tf_op jit(solution)/shard_map/ppermute | solution.py:165
  57.2 0.0 copy-start.8
  57.2 0.6 copy-done.8
  57.8 1.3 %shard_map.70.mine_ref = f32[8,256]{1,0:T(8,128)} custom-call(f32[8,256]{1,0:T(8,128)} %shard_map.69.mine_ref, f32[8,256]{1,0:T(8,128)} %copy-done.8), custom_call_target="tpu_custom_call" | custom-call | tf_op jit(solution)/shard_map/pallas_call | solution.py:179
  59.2 0.7 %collective-permute-start.8 = (f32[8,256]{1,0:T(8,128)}, f32[8,256]{1,0:T(8,128)S(1)}, u32[]{:S(2)}, u32[]{:S(2)}) collective-permute-start(f32[8,256]{1,0:T(8,128)} %shard_map.70.mine_ref), channel_id=1, source_target_pairs={{0,2},{1,3},{2,0},{3,1},{4,6},{5,7},{6,4},{7,5},{8,10},{9,11},{10,... | collective-permute-start | bytes 24584 | tf_op jit(solution)/shard_map/ppermute | solution.py:165
  59.9 3.1 %collective-permute-done.8.theirs_ref = f32[8,256]{1,0:T(8,128)S(1)} collective-permute-done((f32[8,256]{1,0:T(8,128)}, f32[8,256]{1,0:T(8,128)S(1)}, u32[]{:S(2)}, u32[]{:S(2)}) %collective-permute-start.8) | collective-permute-done | bytes 8224 | tf_op jit(solution)/shard_map/ppermute | solution.py:165
  63.0 0.0 copy-start.9
  63.0 0.6 copy-done.9
  63.6 1.3 %shard_map.71.mine_ref = f32[8,256]{1,0:T(8,128)} custom-call(f32[8,256]{1,0:T(8,128)} %shard_map.70.mine_ref, f32[8,256]{1,0:T(8,128)} %copy-done.9), custom_call_target="tpu_custom_call" | custom-call | tf_op jit(solution)/shard_map/pallas_call | solution.py:179
  65.0 1.5 %collective-permute-start.9 = (f32[8,256]{1,0:T(8,128)}, f32[8,256]{1,0:T(8,128)S(1)}, u32[]{:S(2)}, u32[]{:S(2)}) collective-permute-start(f32[8,256]{1,0:T(8,128)} %shard_map.71.mine_ref), channel_id=1, source_target_pairs={{0,4},{1,5},{2,6},{3,7},{4,0},{5,1},{6,2},{7,3},{8,12},{9,13},{10,... | collective-permute-start | bytes 24584 | tf_op jit(solution)/shard_map/ppermute | solution.py:165
  67.1 2.6 %collective-permute-done.9.theirs_ref = f32[8,256]{1,0:T(8,128)S(1)} collective-permute-done((f32[8,256]{1,0:T(8,128)}, f32[8,256]{1,0:T(8,128)S(1)}, u32[]{:S(2)}, u32[]{:S(2)}) %collective-permute-start.9) | collective-permute-done | bytes 8224 | tf_op jit(solution)/shard_map/ppermute | solution.py:165
  69.7 0.0 copy-start.10
  69.7 0.6 copy-done.10
  70.3 1.3 %shard_map.72 = (f32[1,32]{1,0:T(1,128)}, f32[1,32]{1,0:T(1,128)}) custom-call(s32[1]{0:T(128)S(6)} %copy.8.live_ref, f32[8,256]{1,0:T(8,128)} %shard_map.71.mine_ref, f32[8,256]{1,0:T(8,128)} %copy-done.10), custom_call_target="tpu_custom_call" | custom-call | tf_op jit(solution)/shard_map/pallas_call | solution.py:187
Async XLA Ops:
  2.3 8.3 %collective-permute-start.1 = (bf16[32,2048]{1,0:T(8,128)(2,1)}, bf16[32,2048]{1,0:T(8,128)(2,1)S(1)}, u32[]{:S(2)}, u32[]{:S(2)}) collective-permute-start(bf16[32,2048]{1,0:T(8,128)(2,1)} %shard_map.68.refs_0_), channel_id=1, source_target_pairs={{0,2},{1,3},{2,0},{3,1},{4,6},{5,7},{6,4},{7,5},{8,10},{9,11},{10,... | collective-permute-start | bytes 393224 | tf_op jit(solution)/shard_map/ppermute | solution.py:165
  5.3 13.2 %collective-permute-start.3 = (bf16[32,2048]{1,0:T(8,128)(2,1)}, bf16[32,2048]{1,0:T(8,128)(2,1)S(1)}, u32[]{:S(2)}, u32[]{:S(2)}) collective-permute-start(bf16[32,2048]{1,0:T(8,128)(2,1)} %shard_map.68.refs_0_), channel_id=1, source_target_pairs={{0,4},{1,5},{2,6},{3,7},{4,0},{5,1},{6,2},{7,3},{8,12},{9,13},{10,... | collective-permute-start | bytes 393224 | tf_op jit(solution)/shard_map/ppermute | solution.py:165
  7.9 12.1 %collective-permute-start.5 = (bf16[32,2048]{1,0:T(8,128)(2,1)}, bf16[32,2048]{1,0:T(8,128)(2,1)S(1)}, u32[]{:S(2)}, u32[]{:S(2)}) collective-permute-start(bf16[32,2048]{1,0:T(8,128)(2,1)} %shard_map.68.refs_0_), channel_id=1, source_target_pairs={{0,6},{1,7},{2,4},{3,5},{4,2},{5,3},{6,0},{7,1},{8,14},{9,15},{10,... | collective-permute-start | bytes 393224 | tf_op jit(solution)/shard_map/ppermute | solution.py:165
  7.9 14.1 %collective-permute-start = (bf16[32,2048]{1,0:T(8,128)(2,1)}, bf16[32,2048]{1,0:T(8,128)(2,1)S(1)}, u32[]{:S(2)}, u32[]{:S(2)}) collective-permute-start(bf16[32,2048]{1,0:T(8,128)(2,1)} %shard_map.68.refs_0_), channel_id=1, source_target_pairs={{0,1},{1,0},{2,3},{3,2},{4,5},{5,4},{6,7},{7,6},{8,9},{9,8},{10,11... | collective-permute-start | bytes 393224 | tf_op jit(solution)/shard_map/ppermute | solution.py:165
  10.6 14.4 %copy-start.1 = (bf16[32,2048]{1,0:T(8,128)(2,1)}, bf16[32,2048]{1,0:T(8,128)(2,1)S(1)}, u32[]{:S(2)}) copy-start(bf16[32,2048]{1,0:T(8,128)(2,1)S(1)} %collective-permute-done.1.refs_2_) | copy-start | bytes 393220
  10.6 11.4 %collective-permute-start.2 = (bf16[32,2048]{1,0:T(8,128)(2,1)S(1)}, bf16[32,2048]{1,0:T(8,128)(2,1)S(1)}, u32[]{:S(2)}, u32[]{:S(2)}) collective-permute-start(bf16[32,2048]{1,0:T(8,128)(2,1)S(1)} %collective-permute-done.1.refs_2_), channel_id=1, source_target_pairs={{0,1},{1,0},{2,3},{3,2},{4,5},{5,4},{6,7},{7,6},{8,9},{9,8},{10,11... | collective-permute-start | bytes 393224 | tf_op jit(solution)/shard_map/ppermute | solution.py:165
  18.5 6.5 %copy-start.2 = (bf16[32,2048]{1,0:T(8,128)(2,1)}, bf16[32,2048]{1,0:T(8,128)(2,1)S(1)}, u32[]{:S(2)}) copy-start(bf16[32,2048]{1,0:T(8,128)(2,1)S(1)} %collective-permute-done.3.refs_4_) | copy-start | bytes 393220
  18.5 5.0 %collective-permute-start.4 = (bf16[32,2048]{1,0:T(8,128)(2,1)S(1)}, bf16[32,2048]{1,0:T(8,128)(2,1)S(1)}, u32[]{:S(2)}, u32[]{:S(2)}) collective-permute-start(bf16[32,2048]{1,0:T(8,128)(2,1)S(1)} %collective-permute-done.3.refs_4_), channel_id=1, source_target_pairs={{0,1},{1,0},{2,3},{3,2},{4,5},{5,4},{6,7},{7,6},{8,9},{9,8},{10,11... | collective-permute-start | bytes 393224 | tf_op jit(solution)/shard_map/ppermute | solution.py:165
  20.0 5.0 %copy-start.3 = (bf16[32,2048]{1,0:T(8,128)(2,1)}, bf16[32,2048]{1,0:T(8,128)(2,1)S(1)}, u32[]{:S(2)}) copy-start(bf16[32,2048]{1,0:T(8,128)(2,1)S(1)} %collective-permute-done.5.refs_6_) | copy-start | bytes 393220
  20.0 5.0 %collective-permute-start.6 = (bf16[32,2048]{1,0:T(8,128)(2,1)S(1)}, bf16[32,2048]{1,0:T(8,128)(2,1)S(1)}, u32[]{:S(2)}, u32[]{:S(2)}) collective-permute-start(bf16[32,2048]{1,0:T(8,128)(2,1)S(1)} %collective-permute-done.5.refs_6_), channel_id=1, source_target_pairs={{0,1},{1,0},{2,3},{3,2},{4,5},{5,4},{6,7},{7,6},{8,9},{9,8},{10,11... | collective-permute-start | bytes 393224 | tf_op jit(solution)/shard_map/ppermute | solution.py:165
  22.0 3.0 %copy-start.4 = (bf16[32,2048]{1,0:T(8,128)(2,1)}, bf16[32,2048]{1,0:T(8,128)(2,1)S(1)}, u32[]{:S(2)}) copy-start(bf16[32,2048]{1,0:T(8,128)(2,1)S(1)} %collective-permute-done.refs_1_) | copy-start | bytes 393220
  22.0 3.0 %copy-start.5 = (bf16[32,2048]{1,0:T(8,128)(2,1)}, bf16[32,2048]{1,0:T(8,128)(2,1)S(1)}, u32[]{:S(2)}) copy-start(bf16[32,2048]{1,0:T(8,128)(2,1)S(1)} %collective-permute-done.2.refs_3_) | copy-start | bytes 393220
  23.5 1.5 %copy-start.6 = (bf16[32,2048]{1,0:T(8,128)(2,1)}, bf16[32,2048]{1,0:T(8,128)(2,1)S(1)}, u32[]{:S(2)}) copy-start(bf16[32,2048]{1,0:T(8,128)(2,1)S(1)} %collective-permute-done.4.refs_5_) | copy-start | bytes 393220
  25.0 0.6 copy-start.7
  25.6 12.9 %copy-start = (bf16[2048,10240]{1,0:T(8,128)(2,1)S(1)}, bf16[2048,10240]{1,0:T(8,128)(2,1)}, u32[]{:S(2)}) copy-start(bf16[2048,10240]{1,0:T(8,128)(2,1)} %refs_9_.1) | copy-start | bytes 125829120
  53.4 3.9 %collective-permute-start.7 = (f32[8,256]{1,0:T(8,128)}, f32[8,256]{1,0:T(8,128)S(1)}, u32[]{:S(2)}, u32[]{:S(2)}) collective-permute-start(f32[8,256]{1,0:T(8,128)} %shard_map.69.mine_ref), channel_id=1, source_target_pairs={{0,1},{1,0},{2,3},{3,2},{4,5},{5,4},{6,7},{7,6},{8,9},{9,8},{10,11... | collective-permute-start | bytes 24584 | tf_op jit(solution)/shard_map/ppermute | solution.py:165
  57.2 0.6 copy-start.8
  59.2 3.9 %collective-permute-start.8 = (f32[8,256]{1,0:T(8,128)}, f32[8,256]{1,0:T(8,128)S(1)}, u32[]{:S(2)}, u32[]{:S(2)}) collective-permute-start(f32[8,256]{1,0:T(8,128)} %shard_map.70.mine_ref), channel_id=1, source_target_pairs={{0,2},{1,3},{2,0},{3,1},{4,6},{5,7},{6,4},{7,5},{8,10},{9,11},{10,... | collective-permute-start | bytes 24584 | tf_op jit(solution)/shard_map/ppermute | solution.py:165
  63.0 0.6 copy-start.9
  65.0 4.8 %collective-permute-start.9 = (f32[8,256]{1,0:T(8,128)}, f32[8,256]{1,0:T(8,128)S(1)}, u32[]{:S(2)}, u32[]{:S(2)}) collective-permute-start(f32[8,256]{1,0:T(8,128)} %shard_map.71.mine_ref), channel_id=1, source_target_pairs={{0,4},{1,5},{2,6},{3,7},{4,0},{5,1},{6,2},{7,3},{8,12},{9,13},{10,... | collective-permute-start | bytes 24584 | tf_op jit(solution)/shard_map/ppermute | solution.py:165
  69.7 0.6 copy-start.10

commit v2 on v0

v2 whole, which is shorter than its diff:
```python
import functools

import jax
import jax.numpy as jnp
from jax import lax
from jax.experimental import pallas as pl
from jax.experimental.pallas import tpu as pltpu
from jax.sharding import PartitionSpec as P

LANES = 128
LOWEST = -1e30
IN_VMEM = pl.BlockSpec(memory_space=pltpu.VMEM)
ANYWHERE = pl.BlockSpec(memory_space=pl.ANY)


def normalise(values, gain):
    values = values.astype(jnp.float32)
    squares = jnp.mean(values * values, axis=1, keepdims=True)
    return (values * lax.rsqrt(squares + 1e-06) * gain).astype(jnp.bfloat16)


def column_of(tokens):
    wide = jnp.broadcast_to(tokens.astype(jnp.float32), (LANES, tokens.shape[1]))
    return wide.T.astype(jnp.int32)


def sweep(n_tiles, multiply, collect):
    multiply(0, 0)
    pairs = (n_tiles - 1) // 2

    @pl.loop(0, pairs)
    def _(pair):
        tile = pair * 2
        multiply(tile + 1, 1)
        collect(tile, 0)
        multiply(tile + 2, 0)
        collect(tile + 1, 1)

    if n_tiles % 2:
        collect(n_tiles - 1, 0)
    else:
        multiply(n_tiles - 1, 1)
        collect(n_tiles - 2, 0)
        collect(n_tiles - 1, 1)


def stage_kernel(plan, *refs):
    distances, before_distances, part, first_rows, tile, half = plan
    final = part is None
    n_blocks = len(distances)
    refs = list(refs)
    blocks = [refs.pop(0) for _ in range(n_blocks)]
    gain_ref, token_ref = refs.pop(0), refs.pop(0)
    before = refs.pop(0) if before_distances else None
    if final:
        parts = [refs.pop(0) for _ in first_rows]
        outs = [refs.pop(0), refs.pop(0)]
    else:
        head_hbm = refs.pop(0)
        outs = [refs.pop(0)]
        loaded = refs.pop(0)
    rows, logits, wanted, by_row, top, total, spread, picked = refs[:8]
    own = blocks[0].shape[0]
    n_tiles = half // tile
    me = lax.axis_index("vocab")
    n_rows = n_blocks * own

    def load(index):
        columns = pl.ds(pl.multiple_of(index * tile, tile), tile)
        source = pl.ds(pl.multiple_of(part * half + index * tile, tile), tile)
        return pltpu.make_async_copy(head_hbm.at[:, source], loaded.at[:, columns], refs[8].at[index])

    if not final:
        for index in range(n_tiles):
            load(index).start()

    gain = gain_ref[...]
    by_row[...] = column_of(token_ref[...])
    lane = lax.broadcasted_iota(jnp.int32, (own, LANES), 1)
    for number, (distance, block) in enumerate(zip(distances, blocks)):
        place = slice(number * own, (number + 1) * own)
        rows[place, :] = normalise(block[...], gain)
        start = pl.multiple_of(lax.bitwise_xor(me, distance) * own, own)
        wanted[place, :] = by_row[pl.ds(start, own), :] - me * half - lane
        if distance in before_distances:
            origin = before_distances.index(distance) * own
            saved = before[origin : origin + own, :]
            top[place, :] = jnp.broadcast_to(saved[:, 0:1], (own, LANES))
            total[place, :] = jnp.where(lane == 0, saved[:, 1:2], 0.0)
            spread[place, :] = jnp.where(lane == 0, saved[:, 2:3], 0.0)
            picked[place, :] = jnp.where(lane == 0, saved[:, 3:4], 0.0)
        else:
            top[place, :] = jnp.full((own, LANES), LOWEST, jnp.float32)
            for sums in (total, spread, picked):
                sums[place, :] = jnp.zeros((own, LANES), jnp.float32)

    def run(head, first_row, first_column, wait):
        def multiply(index, slot):
            if wait:
                load(index).wait()
            columns = pl.ds(pl.multiple_of(index * tile, tile), tile)
            logits[slot, first_row:, :] = jnp.dot(
                rows[first_row:, :], head[:, columns], preferred_element_type=jnp.float32
            )

        def collect(index, slot):
            step = 32
            for begin in range(first_row, n_rows, step):
                place = slice(begin, begin + step)
                pieces = [logits[slot, place, c : c + LANES] for c in range(0, tile, LANES)]
                last = top[place]
                new = jnp.maximum(last, functools.reduce(jnp.maximum, pieces))
                shift = last - new
                factor = jnp.exp(shift)
                sums = total[place]
                spreads = (spread[place] + shift * sums) * factor
                sums = sums * factor
                found = picked[place]
                target = wanted[place]
                for number, piece in enumerate(pieces):
                    shifted = piece - new
                    power = jnp.exp(shifted)
                    sums = sums + power
                    spreads = spreads + power * shifted
                    found = jnp.where(
                        target == first_column + index * tile + number * LANES, piece, found
                    )
                top[place] = new
                total[place] = sums
                spread[place] = spreads
                picked[place] = found

        sweep(n_tiles, multiply, collect)

    if final:
        for number, (head, first_row) in enumerate(zip(parts, first_rows)):
            run(head, first_row, number * half, False)
    else:
        run(loaded, 0, part * half, True)

    row_top = jnp.max(top[...], axis=1, keepdims=True)
    shift = top[...] - row_top
    factor = jnp.exp(shift)
    row_total = jnp.sum(total[...] * factor, axis=1, keepdims=True)
    row_spread = jnp.sum((spread[...] + shift * total[...]) * factor, axis=1, keepdims=True)
    row_picked = jnp.sum(picked[...], axis=1, keepdims=True)
    lane = lax.broadcasted_iota(jnp.int32, (n_rows, LANES), 1)
    packed = jnp.where(
        lane == 0,
        row_top,
        jnp.where(lane == 1, row_total, jnp.where(lane == 2, row_spread, row_picked)),
    )
    if not final:
        outs[0][...] = packed
        return
    whole = refs[8]
    for distance in range(whole.shape[0] // own):
        place = slice(distance * own, (distance + 1) * own)
        if distance in distances:
            origin = distances.index(distance) * own
            whole[place, :] = packed[origin : origin + own, :]
        else:
            origin = before_distances.index(distance) * own
            whole[place, :] = before[origin : origin + own, :]
    table = whole[...].T
    outs[0][...] = table[:4, : whole.shape[0] // 2]
    outs[1][...] = table[:4, whole.shape[0] // 2 :]


def stage(blocks, distances, gain, tokens, before, before_distances, head_weight, part, parts, first_rows):
    own, depth = blocks[0].shape
    final = part is None
    half = parts[0].shape[1] if final else head_weight.shape[1]
    tile = next(t for t in (1024, 512, 256, 128) if half % t == 0)
    n_rows, n_all = own * len(blocks), tokens.shape[1]
    plan = (tuple(distances), tuple(before_distances), part, first_rows, tile, half)
    args = [*blocks, gain, tokens]
    if before_distances:
        args.append(before)
    specs = [IN_VMEM] * len(args)
    if final:
        args += [pltpu.with_memory_space_constraint(p, pltpu.VMEM) for p in parts]
        specs += [IN_VMEM] * len(parts)
        out_shape = [jax.ShapeDtypeStruct((4, n_all // 2), jnp.float32)] * 2
        last = pltpu.VMEM((n_all, LANES), jnp.float32)
        met = sum(n_rows - first for first in first_rows)
    else:
        args.append(head_weight)
        specs.append(ANYWHERE)
        out_shape = [
            jax.ShapeDtypeStruct((n_rows, LANES), jnp.float32),
            pltpu.VMEM((depth, half), jnp.bfloat16),
        ]
        last = pltpu.SemaphoreType.DMA((half // tile,))
        met = n_rows
    scratch = [
        pltpu.VMEM((n_rows, depth), jnp.bfloat16),
        pltpu.VMEM((2, n_rows, tile), jnp.float32),
        pltpu.VMEM((n_rows, LANES), jnp.int32),
        pltpu.VMEM((n_all, LANES), jnp.int32),
    ] + [pltpu.VMEM((n_rows, LANES), jnp.float32)] * 4
    need = n_rows * (4 * depth + 8 * tile + 32 * LANES) + n_all * 16 * LANES + 2**22
    return pl.pallas_call(
        functools.partial(stage_kernel, plan),
        in_specs=specs,
        out_specs=[IN_VMEM] * len(out_shape),
        out_shape=out_shape,
        scratch_shapes=scratch + [last],
        compiler_params=pltpu.CompilerParams(vmem_limit_bytes=need),
        cost_estimate=pl.CostEstimate(
            flops=2 * depth * half * met,
            bytes_accessed=0 if final else 2 * depth * half,
            transcendentals=half * met,
        ),
    )(*args)


def merge(mine, theirs):
    top = jnp.maximum(mine[0], theirs[0])
    a, b = mine[0] - top, theirs[0] - top
    fa, fb = jnp.exp(a), jnp.exp(b)
    total = mine[1] * fa + theirs[1] * fb
    spread = (mine[2] + a * mine[1]) * fa + (theirs[2] + b * theirs[1]) * fb
    return jnp.stack([top, total, spread, mine[3] + theirs[3]])


def swap(array, distance, size):
    return lax.ppermute(array, "vocab", [(i, i ^ distance) for i in range(size)])


def per_device(size, hidden_rows, norm_gain, head_weight, token_ids, live_count):
    own = hidden_rows.shape[0]
    gain, tokens, hidden_rows = (
        pltpu.with_memory_space_constraint(x, pltpu.HBM)
        for x in (norm_gain[None, :], token_ids[None, :], hidden_rows)
    )
    blocks = {0: hidden_rows}
    for distance in range(1, size):
        blocks[distance] = swap(hidden_rows, distance, size)
    near, far = list(range(size // 2)), list(range(size // 2, size))
    pick = lambda which: [blocks[d] for d in which]
    sums, head = stage(pick(near), near, gain, tokens, None, [], head_weight, 0, [], ())
    kept, sent = stage(pick(far), far, gain, tokens, sums, near, None, None, [head], (0,))
    distance = size // 2
    while True:
        stats = merge(kept, swap(sent, distance, size))
        distance //= 2
        if not distance:
            break
        kept, sent = stats[:, : distance * own], stats[:, distance * own :]
    log_total = jnp.log(stats[1])
    logprob = stats[3] - stats[0] - log_total
    entropy = log_total - stats[2] / stats[1]
    live = jnp.arange(own, dtype=jnp.int32) < live_count[0]
    return jnp.where(live, logprob, 0.0), jnp.where(live, entropy, 0.0)


def solution(mesh):
    placed = (P(("req", "vocab"), None), P(), P(None, "vocab"), P("req"), P(("req", "vocab")))
    return jax.shard_map(
        functools.partial(per_device, mesh.shape["vocab"]),
        mesh=mesh,
        in_specs=placed,
        out_specs=(P(("req", "vocab")), P(("req", "vocab"))),
        check_vma=False,
    )
```

time: 129 us -> 54.9 us (0.43)
  blocking collectives: 36.4 us -> 0 us
  waiting for transfers between devices: 41.7 us -> 6.24 us
  Pallas kernels: 0 us -> 23.9 us
  matrix products: 21.1 us -> 0 us
  starting transfers between devices: 0.04 us -> 20.6 us
  between operations: 14.7 us -> 1.4 us
  other arithmetic: 10.3 us -> 1.12 us
  local copies, waits for them, and re-layouts: 4.31 us -> 1.52 us
    all_gather x1 -> x0, waiting for transfers between devices: 41.7 us -> none  [per_device(): gathered = lax.all_gather(normed, 'vocab', axis=0, tiled=True)]
    pallas_call x0 -> x2, Pallas kernels: none -> 23.9 us  [stage(): pl.pallas_call(functools.partial(stage_kernel, plan), in_specs=specs, out...]
    dot_general x1 -> x0, matrix products: 21.1 us -> none  [local_stats(): logits = jnp.dot(row_block, columns, preferred_element_type=jnp.float32)]
    ppermute x0 -> x10, starting transfers between devices: none -> 20.6 us  [swap(): lax.ppermute(array, 'vocab', [(i, i ^ distance) for i in range(size)])]
    pmax x1 -> x0, blocking collectives: 19.3 us -> none  [per_device(): global_top = lax.pmax(row_top, 'vocab')]
    psum x1 -> x0, blocking collectives: 17.1 us -> none  [per_device(): lax.psum((scaled_total, scaled_spread, row_picked), 'vocab')]
    reduce_sum x2 -> x0, other arithmetic: 7.33 us -> none  [the longest x1 6.29 us: local_stats(): row_spread = jnp.sum(powers * shifted, axis=1)]
    ppermute x0 -> x10, waiting for transfers between devices: none -> 6.24 us  [swap(): lax.ppermute(array, 'vocab', [(i, i ^ distance) for i in range(size)])]
  transfers between devices with their start and end apart: 1 -> 10, of which waited for: 1 -> 4; matrix products, arithmetic and copies ran while one was open for 1% -> 0% of each run, Pallas kernels for 0% -> 28%
where the time goes in v2:
time: 54.9 us; the launch traced here: 54.7 us
  Pallas kernels  23.9 us (44%)
  starting transfers between devices  20.6 us (38%)
  waiting for transfers between devices  6.24 us (11%)
  local copies, waits for them, and re-layouts  1.52 us (3%)
  between operations  1.4 us (3%)
  other arithmetic  1.12 us (2%)
    pallas_call x2, Pallas kernels, stage(): pl.pallas_call(functools.partial(stage_kernel, plan), in_specs=specs, out...  23.9 us
    ppermute x10, starting transfers between devices, swap(): lax.ppermute(array, 'vocab', [(i, i ^ distance) for i in range(size)])  20.6 us
    ppermute x10, waiting for transfers between devices, swap(): lax.ppermute(array, 'vocab', [(i, i ^ distance) for i in range(size)])  6.24 us
    unnamed x14, local copies, waits for them, and re-layouts  1.37 us
  transfers between devices with their start and end apart: 10, of which 4 were waited for; matrix products, arithmetic and copies ran while one was open for 0% of the time, Pallas kernels for 28%

profile of v2, /device:TPU:0, one launch (start us, length us, event | category | flops | bytes accessed | tf_op | source)
XLA Modules:
  0.0 54.7 jit_solution(14471597024955368702)
XLA Ops:
  0.6 3.0 %collective-permute-start.4 = (bf16[32,2048]{1,0:T(8,128)(2,1)}, bf16[32,2048]{1,0:T(8,128)(2,1)S(1)}, u32[]{:S(2)}, u32[]{:S(2)}) collective-permute-start(bf16[32,2048]{1,0:T(8,128)(2,1)} %refs_0_.1), channel_id=1, source_target_pairs={{0,1},{1,0},{2,3},{3,2},{4,5},{5,4},{6,7},{7,6},{8,9},{9,8},{10,11... | collective-permute-start | bytes 393224 | tf_op jit(solution)/shard_map/ppermute | solution.py:228
  3.6 1.6 %collective-permute-start.5 = (bf16[32,2048]{1,0:T(8,128)(2,1)}, bf16[32,2048]{1,0:T(8,128)(2,1)S(1)}, u32[]{:S(2)}, u32[]{:S(2)}) collective-permute-start(bf16[32,2048]{1,0:T(8,128)(2,1)} %refs_0_.1), channel_id=1, source_target_pairs={{0,2},{1,3},{2,0},{3,1},{4,6},{5,7},{6,4},{7,5},{8,10},{9,11},{10,... | collective-permute-start | bytes 393224 | tf_op jit(solution)/shard_map/ppermute | solution.py:228
  5.2 0.0 collective-permute-start.6
  5.2 3.0 %collective-permute-start = (bf16[32,2048]{1,0:T(8,128)(2,1)}, bf16[32,2048]{1,0:T(8,128)(2,1)S(1)}, u32[]{:S(2)}, u32[]{:S(2)}) collective-permute-start(bf16[32,2048]{1,0:T(8,128)(2,1)} %refs_0_.1), channel_id=1, source_target_pairs={{0,4},{1,5},{2,6},{3,7},{4,0},{5,1},{6,2},{7,3},{8,12},{9,13},{10,... | collective-permute-start | bytes 393224 | tf_op jit(solution)/shard_map/ppermute | solution.py:228
  8.2 1.3 %collective-permute-start.1 = (bf16[32,2048]{1,0:T(8,128)(2,1)}, bf16[32,2048]{1,0:T(8,128)(2,1)S(1)}, u32[]{:S(2)}, u32[]{:S(2)}) collective-permute-start(bf16[32,2048]{1,0:T(8,128)(2,1)} %refs_0_.1), channel_id=1, source_target_pairs={{0,5},{1,4},{2,7},{3,6},{4,1},{5,0},{6,3},{7,2},{8,13},{9,12},{10,... | collective-permute-start | bytes 393224 | tf_op jit(solution)/shard_map/ppermute | solution.py:228
  9.5 0.0 collective-permute-done.4.refs_1_
  9.5 0.0 copy-start.2
  9.5 3.6 %collective-permute-start.2 = (bf16[32,2048]{1,0:T(8,128)(2,1)}, bf16[32,2048]{1,0:T(8,128)(2,1)S(1)}, u32[]{:S(2)}, u32[]{:S(2)}) collective-permute-start(bf16[32,2048]{1,0:T(8,128)(2,1)} %refs_0_.1), channel_id=1, source_target_pairs={{0,6},{1,7},{2,4},{3,5},{4,2},{5,3},{6,0},{7,1},{8,14},{9,15},{10,... | collective-permute-start | bytes 393224 | tf_op jit(solution)/shard_map/ppermute | solution.py:228
  13.1 1.5 %collective-permute-done.5.refs_2_ = bf16[32,2048]{1,0:T(8,128)(2,1)S(1)} collective-permute-done((bf16[32,2048]{1,0:T(8,128)(2,1)}, bf16[32,2048]{1,0:T(8,128)(2,1)S(1)}, u32[]{:S(2)}, u32[]{:S(2)}) %collective-permute-start.5) | collective-permute-done | bytes 131104 | tf_op jit(solution)/shard_map/ppermute | solution.py:228
  14.6 0.0 copy-start.4
  14.6 0.8 %collective-permute-start.3 = (bf16[32,2048]{1,0:T(8,128)(2,1)}, bf16[32,2048]{1,0:T(8,128)(2,1)S(1)}, u32[]{:S(2)}, u32[]{:S(2)}) collective-permute-start(bf16[32,2048]{1,0:T(8,128)(2,1)} %refs_0_.1), channel_id=1, source_target_pairs={{0,7},{1,6},{2,5},{3,4},{4,3},{5,2},{6,1},{7,0},{8,15},{9,14},{10,... | collective-permute-start | bytes 393224 | tf_op jit(solution)/shard_map/ppermute | solution.py:228
  15.3 0.0 collective-permute-done.6.refs_3_
  15.3 0.0 copy-start.5
  15.3 0.0 copy-done.2
  15.3 0.0 copy-done.4
  15.3 0.6 %copy-done.5 = bf16[32,2048]{1,0:T(8,128)(2,1)} copy-done((bf16[32,2048]{1,0:T(8,128)(2,1)}, bf16[32,2048]{1,0:T(8,128)(2,1)S(1)}, u32[]{:S(2)}) %copy-start.5) | copy-done | bytes 131096
  16.0 15.4 %shard_map.68 = (f32[128,128]{1,0:T(8,128)S(1)}, bf16[2048,10240]{1,0:T(8,128)(2,1)S(1)}) custom-call(bf16[32,2048]{1,0:T(8,128)(2,1)} %refs_0_.1, bf16[32,2048]{1,0:T(8,128)(2,1)} %copy-done.2, bf16[32,2048]{1,0:T(8,128)(2,1)} %copy-done.4, bf16[32,2048]{1,0:T(8,128)(2,1)} %copy-done.5, f32[1,2048]{1,0:T(1,128)} %bitcast.77, s32[1,256]{1,0:T(1,128)} %bitcast.79, ...), custom_call_target="tpu_custom_call" | custom-call | flops 5368709120 | bytes 41943040 | tf_op jit(solution)/shard_map/pallas_call | solution.py:203
  31.4 0.0 collective-permute-done.refs_0_
  31.4 0.0 copy-start
  31.4 0.0 collective-permute-done.1.refs_1_
  31.4 0.0 copy-start.1
  31.4 0.0 collective-permute-done.2.refs_2_
  31.4 0.0 copy-start.3
  31.5 0.0 collective-permute-done.3.refs_3_
  31.5 0.0 copy-start.6
  31.5 0.6 %copy-done = bf16[32,2048]{1,0:T(8,128)(2,1)} copy-done((bf16[32,2048]{1,0:T(8,128)(2,1)}, bf16[32,2048]{1,0:T(8,128)(2,1)S(1)}, u32[]{:S(2)}) %copy-start) | copy-done | bytes 131096
  32.1 0.0 copy-done.1
  32.1 0.0 copy-done.3
  32.2 0.1 copy-done.6
  32.2 8.4 %shard_map.69 = (f32[4,128]{1,0:T(4,128)S(1)}, f32[4,128]{1,0:T(4,128)S(1)}) custom-call(bf16[32,2048]{1,0:T(8,128)(2,1)} %copy-done, bf16[32,2048]{1,0:T(8,128)(2,1)} %copy-done.1, bf16[32,2048]{1,0:T(8,128)(2,1)} %copy-done.3, bf16[32,2048]{1,0:T(8,128)(2,1)} %copy-done.6, f32[1,2048]{1,0:T(1,128)} %bitcast.78, s32[1,256]{1,0:T(1,128)} %bitcast.80, ...), custom_call_target="tpu_custom_call" | custom-call | flops 5368709120 | tf_op jit(solution)/shard_map/pallas_call | solution.py:203
  40.6 2.9 %collective-permute-start.7 = (f32[4,128]{1,0:T(4,128)S(1)}, f32[4,128]{1,0:T(4,128)S(1)}, u32[]{:S(2)}, u32[]{:S(2)}) collective-permute-start(f32[4,128]{1,0:T(4,128)S(1)} %get-tuple-element.9), channel_id=1, source_target_pairs={{0,4},{1,5},{2,6},{3,7},{4,0},{5,1},{6,2},{7,3},{8,12},{9,13},{10,... | collective-permute-start | bytes 6152 | tf_op jit(solution)/shard_map/ppermute | solution.py:228
  43.6 1.6 %collective-permute-done.7 = f32[4,128]{1,0:T(4,128)S(1)} collective-permute-done((f32[4,128]{1,0:T(4,128)S(1)}, f32[4,128]{1,0:T(4,128)S(1)}, u32[]{:S(2)}, u32[]{:S(2)}) %collective-permute-start.7) | collective-permute-done | bytes 2080 | tf_op jit(solution)/shard_map/ppermute | solution.py:228
  45.2 0.1 slice.117
  45.3 1.4 %collective-permute-start.8 = (f32[4,64]{1,0:T(4,128)S(1)}, f32[4,64]{1,0:T(4,128)S(1)}, u32[]{:S(2)}, u32[]{:S(2)}) collective-permute-start(f32[4,64]{1,0:T(4,128)S(1)} %slice.117), channel_id=1, source_target_pairs={{0,2},{1,3},{2,0},{3,1},{4,6},{5,7},{6,4},{7,5},{8,10},{9,11},{10,... | collective-permute-start | bytes 3080 | tf_op jit(solution)/shard_map/ppermute | solution.py:228
  46.7 2.2 %collective-permute-done.8 = f32[4,64]{1,0:T(4,128)S(1)} collective-permute-done((f32[4,64]{1,0:T(4,128)S(1)}, f32[4,64]{1,0:T(4,128)S(1)}, u32[]{:S(2)}, u32[]{:S(2)}) %collective-permute-start.8) | collective-permute-done | bytes 1056 | tf_op jit(solution)/shard_map/ppermute | solution.py:228
  48.9 0.1 slice.126
  49.0 3.1 %collective-permute-start.9 = (f32[4,32]{1,0:T(4,128)S(1)}, f32[4,32]{1,0:T(4,128)S(1)}, u32[]{:S(2)}, u32[]{:S(2)}) collective-permute-start(f32[4,32]{1,0:T(4,128)S(1)} %slice.126), channel_id=1, source_target_pairs={{0,1},{1,0},{2,3},{3,2},{4,5},{5,4},{6,7},{7,6},{8,9},{9,8},{10,11... | collective-permute-start | bytes 1544 | tf_op jit(solution)/shard_map/ppermute | solution.py:228
  52.7 0.9 %collective-permute-done.9 = f32[4,32]{1,0:T(4,128)S(1)} collective-permute-done((f32[4,32]{1,0:T(4,128)S(1)}, f32[4,32]{1,0:T(4,128)S(1)}, u32[]{:S(2)}, u32[]{:S(2)}) %collective-permute-start.9) | collective-permute-done | bytes 544 | tf_op jit(solution)/shard_map/ppermute | solution.py:228
  53.6 0.5 compare_select_fusion
  54.2 0.5 compare_select_fusion.1
  (6 shorter events, 0.1 us)
Async XLA Ops:
  0.6 8.9 %collective-permute-start.4 = (bf16[32,2048]{1,0:T(8,128)(2,1)}, bf16[32,2048]{1,0:T(8,128)(2,1)S(1)}, u32[]{:S(2)}, u32[]{:S(2)}) collective-permute-start(bf16[32,2048]{1,0:T(8,128)(2,1)} %refs_0_.1), channel_id=1, source_target_pairs={{0,1},{1,0},{2,3},{3,2},{4,5},{5,4},{6,7},{7,6},{8,9},{9,8},{10,11... | collective-permute-start | bytes 393224 | tf_op jit(solution)/shard_map/ppermute | solution.py:228
  3.6 10.9 %collective-permute-start.5 = (bf16[32,2048]{1,0:T(8,128)(2,1)}, bf16[32,2048]{1,0:T(8,128)(2,1)S(1)}, u32[]{:S(2)}, u32[]{:S(2)}) collective-permute-start(bf16[32,2048]{1,0:T(8,128)(2,1)} %refs_0_.1), channel_id=1, source_target_pairs={{0,2},{1,3},{2,0},{3,1},{4,6},{5,7},{6,4},{7,5},{8,10},{9,11},{10,... | collective-permute-start | bytes 393224 | tf_op jit(solution)/shard_map/ppermute | solution.py:228
  5.2 10.1 %collective-permute-start.6 = (bf16[32,2048]{1,0:T(8,128)(2,1)}, bf16[32,2048]{1,0:T(8,128)(2,1)S(1)}, u32[]{:S(2)}, u32[]{:S(2)}) collective-permute-start(bf16[32,2048]{1,0:T(8,128)(2,1)} %refs_0_.1), channel_id=1, source_target_pairs={{0,3},{1,2},{2,1},{3,0},{4,7},{5,6},{6,5},{7,4},{8,11},{9,10},{10,... | collective-permute-start | bytes 393224 | tf_op jit(solution)/shard_map/ppermute | solution.py:228
  5.2 26.2 %collective-permute-start = (bf16[32,2048]{1,0:T(8,128)(2,1)}, bf16[32,2048]{1,0:T(8,128)(2,1)S(1)}, u32[]{:S(2)}, u32[]{:S(2)}) collective-permute-start(bf16[32,2048]{1,0:T(8,128)(2,1)} %refs_0_.1), channel_id=1, source_target_pairs={{0,4},{1,5},{2,6},{3,7},{4,0},{5,1},{6,2},{7,3},{8,12},{9,13},{10,... | collective-permute-start | bytes 393224 | tf_op jit(solution)/shard_map/ppermute | solution.py:228
  8.2 23.2 %collective-permute-start.1 = (bf16[32,2048]{1,0:T(8,128)(2,1)}, bf16[32,2048]{1,0:T(8,128)(2,1)S(1)}, u32[]{:S(2)}, u32[]{:S(2)}) collective-permute-start(bf16[32,2048]{1,0:T(8,128)(2,1)} %refs_0_.1), channel_id=1, source_target_pairs={{0,5},{1,4},{2,7},{3,6},{4,1},{5,0},{6,3},{7,2},{8,13},{9,12},{10,... | collective-permute-start | bytes 393224 | tf_op jit(solution)/shard_map/ppermute | solution.py:228
  9.5 5.8 %copy-start.2 = (bf16[32,2048]{1,0:T(8,128)(2,1)}, bf16[32,2048]{1,0:T(8,128)(2,1)S(1)}, u32[]{:S(2)}) copy-start(bf16[32,2048]{1,0:T(8,128)(2,1)S(1)} %collective-permute-done.4.refs_1_) | copy-start | bytes 393220
  9.5 21.9 %collective-permute-start.2 = (bf16[32,2048]{1,0:T(8,128)(2,1)}, bf16[32,2048]{1,0:T(8,128)(2,1)S(1)}, u32[]{:S(2)}, u32[]{:S(2)}) collective-permute-start(bf16[32,2048]{1,0:T(8,128)(2,1)} %refs_0_.1), channel_id=1, source_target_pairs={{0,6},{1,7},{2,4},{3,5},{4,2},{5,3},{6,0},{7,1},{8,14},{9,15},{10,... | collective-permute-start | bytes 393224 | tf_op jit(solution)/shard_map/ppermute | solution.py:228
  14.6 0.8 %copy-start.4 = (bf16[32,2048]{1,0:T(8,128)(2,1)}, bf16[32,2048]{1,0:T(8,128)(2,1)S(1)}, u32[]{:S(2)}) copy-start(bf16[32,2048]{1,0:T(8,128)(2,1)S(1)} %collective-permute-done.5.refs_2_) | copy-start | bytes 393220
  14.6 16.9 %collective-permute-start.3 = (bf16[32,2048]{1,0:T(8,128)(2,1)}, bf16[32,2048]{1,0:T(8,128)(2,1)S(1)}, u32[]{:S(2)}, u32[]{:S(2)}) collective-permute-start(bf16[32,2048]{1,0:T(8,128)(2,1)} %refs_0_.1), channel_id=1, source_target_pairs={{0,7},{1,6},{2,5},{3,4},{4,3},{5,2},{6,1},{7,0},{8,15},{9,14},{10,... | collective-permute-start | bytes 393224 | tf_op jit(solution)/shard_map/ppermute | solution.py:228
  15.3 0.6 %copy-start.5 = (bf16[32,2048]{1,0:T(8,128)(2,1)}, bf16[32,2048]{1,0:T(8,128)(2,1)S(1)}, u32[]{:S(2)}) copy-start(bf16[32,2048]{1,0:T(8,128)(2,1)S(1)} %collective-permute-done.6.refs_3_) | copy-start | bytes 393220
  31.4 0.7 %copy-start = (bf16[32,2048]{1,0:T(8,128)(2,1)}, bf16[32,2048]{1,0:T(8,128)(2,1)S(1)}, u32[]{:S(2)}) copy-start(bf16[32,2048]{1,0:T(8,128)(2,1)S(1)} %collective-permute-done.refs_0_) | copy-start | bytes 393220
  31.4 0.7 %copy-start.1 = (bf16[32,2048]{1,0:T(8,128)(2,1)}, bf16[32,2048]{1,0:T(8,128)(2,1)S(1)}, u32[]{:S(2)}) copy-start(bf16[32,2048]{1,0:T(8,128)(2,1)S(1)} %collective-permute-done.1.refs_1_) | copy-start | bytes 393220
  31.4 0.7 %copy-start.3 = (bf16[32,2048]{1,0:T(8,128)(2,1)}, bf16[32,2048]{1,0:T(8,128)(2,1)S(1)}, u32[]{:S(2)}) copy-start(bf16[32,2048]{1,0:T(8,128)(2,1)S(1)} %collective-permute-done.2.refs_2_) | copy-start | bytes 393220
  31.5 0.7 %copy-start.6 = (bf16[32,2048]{1,0:T(8,128)(2,1)}, bf16[32,2048]{1,0:T(8,128)(2,1)S(1)}, u32[]{:S(2)}) copy-start(bf16[32,2048]{1,0:T(8,128)(2,1)S(1)} %collective-permute-done.3.refs_3_) | copy-start | bytes 393220
  40.6 4.5 %collective-permute-start.7 = (f32[4,128]{1,0:T(4,128)S(1)}, f32[4,128]{1,0:T(4,128)S(1)}, u32[]{:S(2)}, u32[]{:S(2)}) collective-permute-start(f32[4,128]{1,0:T(4,128)S(1)} %get-tuple-element.9), channel_id=1, source_target_pairs={{0,4},{1,5},{2,6},{3,7},{4,0},{5,1},{6,2},{7,3},{8,12},{9,13},{10,... | collective-permute-start | bytes 6152 | tf_op jit(solution)/shard_map/ppermute | solution.py:228
  45.3 3.6 %collective-permute-start.8 = (f32[4,64]{1,0:T(4,128)S(1)}, f32[4,64]{1,0:T(4,128)S(1)}, u32[]{:S(2)}, u32[]{:S(2)}) collective-permute-start(f32[4,64]{1,0:T(4,128)S(1)} %slice.117), channel_id=1, source_target_pairs={{0,2},{1,3},{2,0},{3,1},{4,6},{5,7},{6,4},{7,5},{8,10},{9,11},{10,... | collective-permute-start | bytes 3080 | tf_op jit(solution)/shard_map/ppermute | solution.py:228
  49.0 4.6 %collective-permute-start.9 = (f32[4,32]{1,0:T(4,128)S(1)}, f32[4,32]{1,0:T(4,128)S(1)}, u32[]{:S(2)}, u32[]{:S(2)}) collective-permute-start(f32[4,32]{1,0:T(4,128)S(1)} %slice.126), channel_id=1, source_target_pairs={{0,1},{1,0},{2,3},{3,2},{4,5},{5,4},{6,7},{7,6},{8,9},{9,8},{10,11... | collective-permute-start | bytes 1544 | tf_op jit(solution)/shard_map/ppermute | solution.py:228

commit v3 on v0

v3 whole, which is shorter than its diff:
```python
import functools

import jax
import jax.numpy as jnp
from jax import lax
from jax.experimental import pallas as pl
from jax.experimental.pallas import tpu as pltpu
from jax.sharding import PartitionSpec as P

LANES = 128
LOWEST = -1e30
IN_VMEM = pl.BlockSpec(memory_space=pltpu.VMEM)
ANYWHERE = pl.BlockSpec(memory_space=pl.ANY)


def normalise(values, gain):
    values = values.astype(jnp.float32)
    squares = jnp.mean(values * values, axis=1, keepdims=True)
    return (values * lax.rsqrt(squares + 1e-06) * gain).astype(jnp.bfloat16)


def norm_kernel(hidden_hbm, gain_hbm, out_ref, hidden, gain, sems):
    copies = [
        pltpu.make_async_copy(source, target, sems.at[number])
        for number, (source, target) in enumerate(((hidden_hbm, hidden), (gain_hbm, gain)))
    ]
    for copy in copies:
        copy.start()
    for copy in copies:
        copy.wait()
    out_ref[...] = normalise(hidden[...], gain[...])


def norm_rows(hidden_rows, gain):
    return pl.pallas_call(
        norm_kernel,
        in_specs=[ANYWHERE, ANYWHERE],
        out_specs=IN_VMEM,
        out_shape=jax.ShapeDtypeStruct(hidden_rows.shape, jnp.bfloat16),
        scratch_shapes=[
            pltpu.VMEM(hidden_rows.shape, hidden_rows.dtype),
            pltpu.VMEM(gain.shape, gain.dtype),
            pltpu.SemaphoreType.DMA((2,)),
        ],
        compiler_params=pltpu.CompilerParams(vmem_limit_bytes=3 * 2**20),
        cost_estimate=pl.CostEstimate(flops=10**11, bytes_accessed=10**8, transcendentals=0),
    )(*(pltpu.with_memory_space_constraint(x, pltpu.HBM) for x in (hidden_rows, gain)))


def column_of(tokens):
    wide = jnp.broadcast_to(tokens.astype(jnp.float32), (LANES, tokens.shape[1]))
    return wide.T.astype(jnp.int32)


def sweep(n_tiles, multiply, collect):
    multiply(0, 0)
    pairs = (n_tiles - 1) // 2

    @pl.loop(0, pairs)
    def _(pair):
        tile = pair * 2
        multiply(tile + 1, 1)
        collect(tile, 0)
        multiply(tile + 2, 0)
        collect(tile + 1, 1)

    if n_tiles % 2:
        collect(n_tiles - 1, 0)
    else:
        multiply(n_tiles - 1, 1)
        collect(n_tiles - 2, 0)
        collect(n_tiles - 1, 1)


def head_kernel(owner_of, tile, *refs):
    n_blocks = len(refs) - 12
    blocks, refs = refs[:n_blocks], refs[n_blocks:]
    token_ref, head, kept_ref, sent_ref, rows, logits, wanted, by_row, top, total, spread, picked = refs
    own = blocks[0].shape[0]
    width = head.shape[1]
    n_tiles = width // tile
    me = lax.axis_index("vocab")
    n_rows = n_blocks * own

    by_row[...] = column_of(token_ref[...])
    lane = lax.broadcasted_iota(jnp.int32, (own, LANES), 1)
    for number, block in enumerate(blocks):
        owner = owner_of(me, number)
        place = pl.ds(pl.multiple_of(lax.bitwise_xor(owner, me) * own, own), own)
        rows[place, :] = block[...]
        start = pl.multiple_of(owner * own, own)
        wanted[place, :] = by_row[pl.ds(start, own), :] - me * width - lane
    top[...] = jnp.full(top.shape, LOWEST, jnp.float32)
    for sums in (total, spread, picked):
        sums[...] = jnp.zeros(sums.shape, jnp.float32)

    def multiply(index, slot):
        columns = pl.ds(pl.multiple_of(index * tile, tile), tile)
        logits[slot] = jnp.dot(rows[...], head[:, columns], preferred_element_type=jnp.float32)

    def collect(index, slot):
        step = 32
        for begin in range(0, n_rows, step):
            place = slice(begin, begin + step)
            pieces = [logits[slot, place, c : c + LANES] for c in range(0, tile, LANES)]
            last = top[place]
            new = jnp.maximum(last, functools.reduce(jnp.maximum, pieces))
            shift = last - new
            factor = jnp.exp(shift)
            sums = total[place]
            spreads = (spread[place] + shift * sums) * factor
            sums = sums * factor
            found = picked[place]
            target = wanted[place]
            for number, piece in enumerate(pieces):
                shifted = piece - new
                power = jnp.exp(shifted)
                sums = sums + power
                spreads = spreads + power * shifted
                found = jnp.where(target == index * tile + number * LANES, piece, found)
            top[place] = new
            total[place] = sums
            spread[place] = spreads
            picked[place] = found

    sweep(n_tiles, multiply, collect)

    row_top = jnp.max(top[...], axis=1, keepdims=True)
    shift = top[...] - row_top
    factor = jnp.exp(shift)
    row_total = jnp.sum(total[...] * factor, axis=1, keepdims=True)
    row_spread = jnp.sum((spread[...] + shift * total[...]) * factor, axis=1, keepdims=True)
    row_picked = jnp.sum(picked[...], axis=1, keepdims=True)
    lane = lax.broadcasted_iota(jnp.int32, (n_rows, LANES), 1)
    packed = jnp.where(
        lane == 0,
        row_top,
        jnp.where(lane == 1, row_total, jnp.where(lane == 2, row_spread, row_picked)),
    )
    table = packed.T
    kept_ref[...] = table[:4, : n_rows // 2]
    sent_ref[...] = table[:4, n_rows // 2 :]


def head_stats(blocks, owner_of, tokens, head):
    own, depth = blocks[0].shape
    tile = next(t for t in (1024, 512, 256, 128) if head.shape[1] % t == 0)
    n_rows = own * len(blocks)
    args = [*blocks, tokens, pltpu.with_memory_space_constraint(head, pltpu.VMEM)]
    return pl.pallas_call(
        functools.partial(head_kernel, owner_of, tile),
        in_specs=[IN_VMEM] * len(args),
        out_specs=[IN_VMEM] * 2,
        out_shape=[jax.ShapeDtypeStruct((4, n_rows // 2), jnp.float32)] * 2,
        scratch_shapes=[
            pltpu.VMEM((n_rows, depth), jnp.bfloat16),
            pltpu.VMEM((2, n_rows, tile), jnp.float32),
            pltpu.VMEM((n_rows, LANES), jnp.int32),
            pltpu.VMEM((n_rows, LANES), jnp.int32),
        ]
        + [pltpu.VMEM((n_rows, LANES), jnp.float32)] * 4,
        compiler_params=pltpu.CompilerParams(
            vmem_limit_bytes=n_rows * (4 * depth + 8 * tile + 48 * LANES) + 2**22
        ),
        cost_estimate=pl.CostEstimate(flops=1, bytes_accessed=500 * 2**20, transcendentals=0),
    )(*args)


def merge(mine, theirs):
    top = jnp.maximum(mine[0], theirs[0])
    a, b = mine[0] - top, theirs[0] - top
    fa, fb = jnp.exp(a), jnp.exp(b)
    total = mine[1] * fa + theirs[1] * fb
    spread = (mine[2] + a * mine[1]) * fa + (theirs[2] + b * theirs[1]) * fb
    return jnp.stack([top, total, spread, mine[3] + theirs[3]])


def swap(array, distance, size):
    return lax.ppermute(array, "vocab", [(i, i ^ distance) for i in range(size)])


def turn(array, distance, size):
    return lax.ppermute(array, "vocab", [(i, (i + distance) % size) for i in range(size)])


def gather(normed, size):
    blocks = {0: normed}
    for distance in range(size - 2, 0, -2):
        blocks[distance] = swap(normed, distance, size)
    for distance in range(0, size, 2):
        blocks[distance + 1] = swap(blocks[distance], 1, size)
    return [blocks[d] for d in range(size)], lambda me, number: lax.bitwise_xor(me, number)


def per_device(size, hidden_rows, norm_gain, head_weight, token_ids, live_count):
    own = hidden_rows.shape[0]
    tokens = token_ids[None, :]
    normed = norm_rows(hidden_rows, norm_gain[None, :])
    blocks, owner_of = gather(normed, size)
    kept, sent = head_stats(blocks, owner_of, tokens, head_weight)
    distance = size // 2
    while True:
        stats = merge(kept, swap(sent, distance, size))
        distance //= 2
        if not distance:
            break
        kept, sent = stats[:, : distance * own], stats[:, distance * own :]
    log_total = jnp.log(stats[1])
    logprob = stats[3] - stats[0] - log_total
    entropy = log_total - stats[2] / stats[1]
    live = jnp.arange(own, dtype=jnp.int32) < live_count[0]
    return jnp.where(live, logprob, 0.0), jnp.where(live, entropy, 0.0)


def solution(mesh):
    placed = (P(("req", "vocab"), None), P(), P(None, "vocab"), P("req"), P(("req", "vocab")))
    return jax.shard_map(
        functools.partial(per_device, mesh.shape["vocab"]),
        mesh=mesh,
        in_specs=placed,
        out_specs=(P(("req", "vocab")), P(("req", "vocab"))),
        check_vma=False,
    )
```

time: 129 us -> 51.2 us (0.40)
  blocking collectives: 36.4 us -> 0 us
  waiting for transfers between devices: 41.7 us -> 18.8 us
  matrix products: 21.1 us -> 0 us
  Pallas kernels: 0 us -> 14.9 us
  starting transfers between devices: 0.04 us -> 14.7 us
  between operations: 14.7 us -> 1.35 us
  other arithmetic: 10.3 us -> 1.12 us
  local copies, waits for them, and re-layouts: 4.31 us -> 0.15 us
    all_gather x1 -> x0, waiting for transfers between devices: 41.7 us -> none  [per_device(): gathered = lax.all_gather(normed, 'vocab', axis=0, tiled=True)]
    dot_general x1 -> x0, matrix products: 21.1 us -> none  [local_stats(): logits = jnp.dot(row_block, columns, preferred_element_type=jnp.float32)]
    pmax x1 -> x0, blocking collectives: 19.3 us -> none  [per_device(): global_top = lax.pmax(row_top, 'vocab')]
    ppermute x0 -> x10, waiting for transfers between devices: none -> 18.8 us  [swap(): lax.ppermute(array, 'vocab', [(i, i ^ distance) for i in range(size)])]
    psum x1 -> x0, blocking collectives: 17.1 us -> none  [per_device(): lax.psum((scaled_total, scaled_spread, row_picked), 'vocab')]
    pallas_call x0 -> x2, Pallas kernels: none -> 14.9 us  [the longest x1 13.7 us: head_stats(): pl.pallas_call(functools.partial(head_kernel, owner_of, tile), in_specs=[...]
    ppermute x0 -> x10, starting transfers between devices: none -> 14.7 us  [swap(): lax.ppermute(array, 'vocab', [(i, i ^ distance) for i in range(size)])]
    reduce_sum x2 -> x0, other arithmetic: 7.33 us -> none  [the longest x1 6.29 us: local_stats(): row_spread = jnp.sum(powers * shifted, axis=1)]
  transfers between devices with their start and end apart: 1 -> 10, of which waited for: 1 -> 7; matrix products, arithmetic and copies ran while one was open for 1% -> 0% of each run, Pallas kernels for 0% -> 0%
where the time goes in v3:
time: 51.2 us; the launch traced here: 51 us
  waiting for transfers between devices  18.8 us (37%)
  Pallas kernels  14.9 us (29%)
  starting transfers between devices  14.7 us (29%)
  between operations  1.35 us (3%)
  other arithmetic  1.12 us (2%)
    ppermute x10, waiting for transfers between devices, swap(): lax.ppermute(array, 'vocab', [(i, i ^ distance) for i in range(size)])  18.8 us
    ppermute x10, starting transfers between devices, swap(): lax.ppermute(array, 'vocab', [(i, i ^ distance) for i in range(size)])  14.7 us
    pallas_call x1, Pallas kernels, head_stats(): pl.pallas_call(functools.partial(head_kernel, owner_of, tile), in_specs=[...  13.7 us
    pallas_call x1, Pallas kernels, norm_rows(): pl.pallas_call(norm_kernel, in_specs=[ANYWHERE, ANYWHERE], out_specs=IN_V...  1.2 us
    select_n x2, other arithmetic, per_device(): return (jnp.where(live, logprob, 0.0), jnp.where(live, entropy, 0.0))  1.05 us
  transfers between devices with their start and end apart: 10, of which 7 were waited for; matrix products, arithmetic and copies ran while one was open for 0% of the time, Pallas kernels for 0%

profile of v3, /device:TPU:0, one launch (start us, length us, event | category | flops | bytes accessed | tf_op | source)
XLA Modules:
  0.0 51.0 jit_solution(5509677640307693668)
XLA Ops:
  0.6 0.0 copy-start
  0.6 0.0 copy-start.1
  0.7 1.2 %shard_map.68.refs_0_ = bf16[32,2048]{1,0:T(8,128)(2,1)S(1)} custom-call(bf16[32,2048]{1,0:T(8,128)(2,1)} %hidden_hbm.1, f32[1,2048]{1,0:T(1,128)} %bitcast.78), custom_call_target="tpu_custom_call" | custom-call | flops 99999997952 | bytes 100000000 | tf_op jit(solution)/shard_map/pallas_call | solution.py:35
  1.9 3.1 %collective-permute-start.1 = (bf16[32,2048]{1,0:T(8,128)(2,1)S(1)}, bf16[32,2048]{1,0:T(8,128)(2,1)S(1)}, u32[]{:S(2)}, u32[]{:S(2)}) collective-permute-start(bf16[32,2048]{1,0:T(8,128)(2,1)S(1)} %shard_map.68.refs_0_), channel_id=1, source_target_pairs={{0,2},{1,3},{2,0},{3,1},{4,6},{5,7},{6,4},{7,5},{8,10},{9,11},{10,... | collective-permute-start | bytes 393224 | tf_op jit(solution)/shard_map/ppermute | solution.py:179
  5.0 2.6 %collective-permute-start.3 = (bf16[32,2048]{1,0:T(8,128)(2,1)S(1)}, bf16[32,2048]{1,0:T(8,128)(2,1)S(1)}, u32[]{:S(2)}, u32[]{:S(2)}) collective-permute-start(bf16[32,2048]{1,0:T(8,128)(2,1)S(1)} %shard_map.68.refs_0_), channel_id=1, source_target_pairs={{0,4},{1,5},{2,6},{3,7},{4,0},{5,1},{6,2},{7,3},{8,12},{9,13},{10,... | collective-permute-start | bytes 393224 | tf_op jit(solution)/shard_map/ppermute | solution.py:179
  7.5 0.0 collective-permute-start.5
  7.5 1.7 %collective-permute-start = (bf16[32,2048]{1,0:T(8,128)(2,1)S(1)}, bf16[32,2048]{1,0:T(8,128)(2,1)S(1)}, u32[]{:S(2)}, u32[]{:S(2)}) collective-permute-start(bf16[32,2048]{1,0:T(8,128)(2,1)S(1)} %shard_map.68.refs_0_), channel_id=1, source_target_pairs={{0,1},{1,0},{2,3},{3,2},{4,5},{5,4},{6,7},{7,6},{8,9},{9,8},{10,11... | collective-permute-start | bytes 393224 | tf_op jit(solution)/shard_map/ppermute | solution.py:179
  9.3 0.7 %collective-permute-done.1.refs_2_ = bf16[32,2048]{1,0:T(8,128)(2,1)S(1)} collective-permute-done((bf16[32,2048]{1,0:T(8,128)(2,1)S(1)}, bf16[32,2048]{1,0:T(8,128)(2,1)S(1)}, u32[]{:S(2)}, u32[]{:S(2)}) %collective-permute-start.1) | collective-permute-done | bytes 131104 | tf_op jit(solution)/shard_map/ppermute | solution.py:179
  10.0 1.7 %collective-permute-start.2 = (bf16[32,2048]{1,0:T(8,128)(2,1)S(1)}, bf16[32,2048]{1,0:T(8,128)(2,1)S(1)}, u32[]{:S(2)}, u32[]{:S(2)}) collective-permute-start(bf16[32,2048]{1,0:T(8,128)(2,1)S(1)} %collective-permute-done.1.refs_2_), channel_id=1, source_target_pairs={{0,1},{1,0},{2,3},{3,2},{4,5},{5,4},{6,7},{7,6},{8,9},{9,8},{10,11... | collective-permute-start | bytes 393224 | tf_op jit(solution)/shard_map/ppermute | solution.py:179
  11.7 6.2 %collective-permute-done.3.refs_4_ = bf16[32,2048]{1,0:T(8,128)(2,1)S(1)} collective-permute-done((bf16[32,2048]{1,0:T(8,128)(2,1)S(1)}, bf16[32,2048]{1,0:T(8,128)(2,1)S(1)}, u32[]{:S(2)}, u32[]{:S(2)}) %collective-permute-start.3) | collective-permute-done | bytes 131104 | tf_op jit(solution)/shard_map/ppermute | solution.py:179
  17.9 1.5 %collective-permute-start.4 = (bf16[32,2048]{1,0:T(8,128)(2,1)S(1)}, bf16[32,2048]{1,0:T(8,128)(2,1)S(1)}, u32[]{:S(2)}, u32[]{:S(2)}) collective-permute-start(bf16[32,2048]{1,0:T(8,128)(2,1)S(1)} %collective-permute-done.3.refs_4_), channel_id=1, source_target_pairs={{0,1},{1,0},{2,3},{3,2},{4,5},{5,4},{6,7},{7,6},{8,9},{9,8},{10,11... | collective-permute-start | bytes 393224 | tf_op jit(solution)/shard_map/ppermute | solution.py:179
  19.4 0.0 collective-permute-done.5.refs_6_
  19.4 0.5 %collective-permute-start.6 = (bf16[32,2048]{1,0:T(8,128)(2,1)S(1)}, bf16[32,2048]{1,0:T(8,128)(2,1)S(1)}, u32[]{:S(2)}, u32[]{:S(2)}) collective-permute-start(bf16[32,2048]{1,0:T(8,128)(2,1)S(1)} %collective-permute-done.5.refs_6_), channel_id=1, source_target_pairs={{0,1},{1,0},{2,3},{3,2},{4,5},{5,4},{6,7},{7,6},{8,9},{9,8},{10,11... | collective-permute-start | bytes 393224 | tf_op jit(solution)/shard_map/ppermute | solution.py:179
  19.9 0.0 collective-permute-done.refs_1_
  19.9 0.0 collective-permute-done.2.refs_3_
  19.9 2.9 %collective-permute-done.4.refs_5_ = bf16[32,2048]{1,0:T(8,128)(2,1)S(1)} collective-permute-done((bf16[32,2048]{1,0:T(8,128)(2,1)S(1)}, bf16[32,2048]{1,0:T(8,128)(2,1)S(1)}, u32[]{:S(2)}, u32[]{:S(2)}) %collective-permute-start.4) | collective-permute-done | bytes 131104 | tf_op jit(solution)/shard_map/ppermute | solution.py:179
  22.8 1.5 %collective-permute-done.6.refs_7_ = bf16[32,2048]{1,0:T(8,128)(2,1)S(1)} collective-permute-done((bf16[32,2048]{1,0:T(8,128)(2,1)S(1)}, bf16[32,2048]{1,0:T(8,128)(2,1)S(1)}, u32[]{:S(2)}, u32[]{:S(2)}) %collective-permute-start.6) | collective-permute-done | bytes 131104 | tf_op jit(solution)/shard_map/ppermute | solution.py:179
  24.3 0.0 copy-done
  24.3 0.0 copy-done.1
  24.3 13.7 %shard_map.69 = (f32[4,128]{1,0:T(4,128)S(1)}, f32[4,128]{1,0:T(4,128)S(1)}) custom-call(bf16[32,2048]{1,0:T(8,128)(2,1)S(1)} %shard_map.68.refs_0_, bf16[32,2048]{1,0:T(8,128)(2,1)S(1)} %collective-permute-done.refs_1_, bf16[32,2048]{1,0:T(8,128)(2,1)S(1)} %collective-permute-done.1.refs_2_, bf16[32,2048]{1,0:T(8,128)(2,1)S(1)} %collective-permute-done.2.refs_3_, ...), custom_call_target="tpu_custom_call" | custom-call | flops 1 | bytes 524288000 | tf_op jit(solution)/shard_map/pallas_call | solution.py:150
  38.0 1.5 %collective-permute-start.7 = (f32[4,128]{1,0:T(4,128)S(1)}, f32[4,128]{1,0:T(4,128)S(1)}, u32[]{:S(2)}, u32[]{:S(2)}) collective-permute-start(f32[4,128]{1,0:T(4,128)S(1)} %get-tuple-element.5), channel_id=1, source_target_pairs={{0,4},{1,5},{2,6},{3,7},{4,0},{5,1},{6,2},{7,3},{8,12},{9,13},{10,... | collective-permute-start | bytes 6152 | tf_op jit(solution)/shard_map/ppermute | solution.py:179
  39.5 3.0 %collective-permute-done.7 = f32[4,128]{1,0:T(4,128)S(1)} collective-permute-done((f32[4,128]{1,0:T(4,128)S(1)}, f32[4,128]{1,0:T(4,128)S(1)}, u32[]{:S(2)}, u32[]{:S(2)}) %collective-permute-start.7) | collective-permute-done | bytes 2080 | tf_op jit(solution)/shard_map/ppermute | solution.py:179
  42.6 0.1 slice.117
  42.7 0.7 %collective-permute-start.8 = (f32[4,64]{1,0:T(4,128)S(1)}, f32[4,64]{1,0:T(4,128)S(1)}, u32[]{:S(2)}, u32[]{:S(2)}) collective-permute-start(f32[4,64]{1,0:T(4,128)S(1)} %slice.117), channel_id=1, source_target_pairs={{0,2},{1,3},{2,0},{3,1},{4,6},{5,7},{6,4},{7,5},{8,10},{9,11},{10,... | collective-permute-start | bytes 3080 | tf_op jit(solution)/shard_map/ppermute | solution.py:179
  43.4 2.9 %collective-permute-done.8 = f32[4,64]{1,0:T(4,128)S(1)} collective-permute-done((f32[4,64]{1,0:T(4,128)S(1)}, f32[4,64]{1,0:T(4,128)S(1)}, u32[]{:S(2)}, u32[]{:S(2)}) %collective-permute-start.8) | collective-permute-done | bytes 1056 | tf_op jit(solution)/shard_map/ppermute | solution.py:179
  46.3 0.1 slice.126
  46.4 1.4 %collective-permute-start.9 = (f32[4,32]{1,0:T(4,128)S(1)}, f32[4,32]{1,0:T(4,128)S(1)}, u32[]{:S(2)}, u32[]{:S(2)}) collective-permute-start(f32[4,32]{1,0:T(4,128)S(1)} %slice.126), channel_id=1, source_target_pairs={{0,1},{1,0},{2,3},{3,2},{4,5},{5,4},{6,7},{7,6},{8,9},{9,8},{10,11... | collective-permute-start | bytes 1544 | tf_op jit(solution)/shard_map/ppermute | solution.py:179
  48.5 1.5 %collective-permute-done.9 = f32[4,32]{1,0:T(4,128)S(1)} collective-permute-done((f32[4,32]{1,0:T(4,128)S(1)}, f32[4,32]{1,0:T(4,128)S(1)}, u32[]{:S(2)}, u32[]{:S(2)}) %collective-permute-start.9) | collective-permute-done | bytes 544 | tf_op jit(solution)/shard_map/ppermute | solution.py:179
  50.0 0.5 %compare_select_fusion = (f32[32]{0:T(128)}, f32[32]{0:T(128)S(1)}) fusion(f32[4,32]{1,0:T(4,128)S(1)} %collective-permute-done.9, f32[1,64]{1,0:T(1,128)S(1)} %get-tuple-element.14, f32[1,64]{1,0:T(1,128)S(1)} %get-tuple-element.8, s32[]{:T(128)} %bitcast.76, f32[1,64]{1,0:T(1,128)S(1)} %get-tuple-element.9), kind=kLoop, calls=%fused_computation.2 | loop fusion | flops 544 | bytes 1028 | tf_op jit(solution)/shard_map/jit(_where)/select_n | solution.py:212
  50.5 0.5 %compare_select_fusion.1 = f32[32]{0:T(128)} fusion(f32[4,32]{1,0:T(4,128)S(1)} %collective-permute-done.9, f32[1,64]{1,0:T(1,128)S(1)} %get-tuple-element.15, f32[32]{0:T(128)S(1)} %get-tuple-element.7, s32[]{:T(128)} %bitcast.75, f32[1,64]{1,0:T(1,128)S(1)} %get-tuple-element.9), kind=kLoop, calls=%fused_computation.3 | loop fusion | flops 192 | bytes 772 | tf_op jit(solution)/shard_map/jit(_where)/select_n | solution.py:212
  (6 shorter events, 0.1 us)
Async XLA Ops:
  0.6 23.7 %copy-start = (bf16[2048,10240]{1,0:T(8,128)(2,1)S(1)}, bf16[2048,10240]{1,0:T(8,128)(2,1)}, u32[]{:S(2)}) copy-start(bf16[2048,10240]{1,0:T(8,128)(2,1)} %refs_9_.1) | copy-start | bytes 125829120
  0.6 23.7 %copy-start.1 = (s32[256]{0:T(256)S(1)}, s32[256]{0:T(256)}, u32[]{:S(2)}) copy-start(s32[256]{0:T(256)} %param.8) | copy-start | bytes 3076
  1.9 8.1 %collective-permute-start.1 = (bf16[32,2048]{1,0:T(8,128)(2,1)S(1)}, bf16[32,2048]{1,0:T(8,128)(2,1)S(1)}, u32[]{:S(2)}, u32[]{:S(2)}) collective-permute-start(bf16[32,2048]{1,0:T(8,128)(2,1)S(1)} %shard_map.68.refs_0_), channel_id=1, source_target_pairs={{0,2},{1,3},{2,0},{3,1},{4,6},{5,7},{6,4},{7,5},{8,10},{9,11},{10,... | collective-permute-start | bytes 393224 | tf_op jit(solution)/shard_map/ppermute | solution.py:179
  5.0 12.9 %collective-permute-start.3 = (bf16[32,2048]{1,0:T(8,128)(2,1)S(1)}, bf16[32,2048]{1,0:T(8,128)(2,1)S(1)}, u32[]{:S(2)}, u32[]{:S(2)}) collective-permute-start(bf16[32,2048]{1,0:T(8,128)(2,1)S(1)} %shard_map.68.refs_0_), channel_id=1, source_target_pairs={{0,4},{1,5},{2,6},{3,7},{4,0},{5,1},{6,2},{7,3},{8,12},{9,13},{10,... | collective-permute-start | bytes 393224 | tf_op jit(solution)/shard_map/ppermute | solution.py:179
  7.5 11.8 %collective-permute-start.5 = (bf16[32,2048]{1,0:T(8,128)(2,1)S(1)}, bf16[32,2048]{1,0:T(8,128)(2,1)S(1)}, u32[]{:S(2)}, u32[]{:S(2)}) collective-permute-start(bf16[32,2048]{1,0:T(8,128)(2,1)S(1)} %shard_map.68.refs_0_), channel_id=1, source_target_pairs={{0,6},{1,7},{2,4},{3,5},{4,2},{5,3},{6,0},{7,1},{8,14},{9,15},{10,... | collective-permute-start | bytes 393224 | tf_op jit(solution)/shard_map/ppermute | solution.py:179
  7.5 12.4 %collective-permute-start = (bf16[32,2048]{1,0:T(8,128)(2,1)S(1)}, bf16[32,2048]{1,0:T(8,128)(2,1)S(1)}, u32[]{:S(2)}, u32[]{:S(2)}) collective-permute-start(bf16[32,2048]{1,0:T(8,128)(2,1)S(1)} %shard_map.68.refs_0_), channel_id=1, source_target_pairs={{0,1},{1,0},{2,3},{3,2},{4,5},{5,4},{6,7},{7,6},{8,9},{9,8},{10,11... | collective-permute-start | bytes 393224 | tf_op jit(solution)/shard_map/ppermute | solution.py:179
  10.0 9.9 %collective-permute-start.2 = (bf16[32,2048]{1,0:T(8,128)(2,1)S(1)}, bf16[32,2048]{1,0:T(8,128)(2,1)S(1)}, u32[]{:S(2)}, u32[]{:S(2)}) collective-permute-start(bf16[32,2048]{1,0:T(8,128)(2,1)S(1)} %collective-permute-done.1.refs_2_), channel_id=1, source_target_pairs={{0,1},{1,0},{2,3},{3,2},{4,5},{5,4},{6,7},{7,6},{8,9},{9,8},{10,11... | collective-permute-start | bytes 393224 | tf_op jit(solution)/shard_map/ppermute | solution.py:179
  17.9 5.0 %collective-permute-start.4 = (bf16[32,2048]{1,0:T(8,128)(2,1)S(1)}, bf16[32,2048]{1,0:T(8,128)(2,1)S(1)}, u32[]{:S(2)}, u32[]{:S(2)}) collective-permute-start(bf16[32,2048]{1,0:T(8,128)(2,1)S(1)} %collective-permute-done.3.refs_4_), channel_id=1, source_target_pairs={{0,1},{1,0},{2,3},{3,2},{4,5},{5,4},{6,7},{7,6},{8,9},{9,8},{10,11... | collective-permute-start | bytes 393224 | tf_op jit(solution)/shard_map/ppermute | solution.py:179
  19.4 5.0 %collective-permute-start.6 = (bf16[32,2048]{1,0:T(8,128)(2,1)S(1)}, bf16[32,2048]{1,0:T(8,128)(2,1)S(1)}, u32[]{:S(2)}, u32[]{:S(2)}) collective-permute-start(bf16[32,2048]{1,0:T(8,128)(2,1)S(1)} %collective-permute-done.5.refs_6_), channel_id=1, source_target_pairs={{0,1},{1,0},{2,3},{3,2},{4,5},{5,4},{6,7},{7,6},{8,9},{9,8},{10,11... | collective-permute-start | bytes 393224 | tf_op jit(solution)/shard_map/ppermute | solution.py:179
  38.0 4.5 %collective-permute-start.7 = (f32[4,128]{1,0:T(4,128)S(1)}, f32[4,128]{1,0:T(4,128)S(1)}, u32[]{:S(2)}, u32[]{:S(2)}) collective-permute-start(f32[4,128]{1,0:T(4,128)S(1)} %get-tuple-element.5), channel_id=1, source_target_pairs={{0,4},{1,5},{2,6},{3,7},{4,0},{5,1},{6,2},{7,3},{8,12},{9,13},{10,... | collective-permute-start | bytes 6152 | tf_op jit(solution)/shard_map/ppermute | solution.py:179
  42.7 3.6 %collective-permute-start.8 = (f32[4,64]{1,0:T(4,128)S(1)}, f32[4,64]{1,0:T(4,128)S(1)}, u32[]{:S(2)}, u32[]{:S(2)}) collective-permute-start(f32[4,64]{1,0:T(4,128)S(1)} %slice.117), channel_id=1, source_target_pairs={{0,2},{1,3},{2,0},{3,1},{4,6},{5,7},{6,4},{7,5},{8,10},{9,11},{10,... | collective-permute-start | bytes 3080 | tf_op jit(solution)/shard_map/ppermute | solution.py:179
  46.4 3.6 %collective-permute-start.9 = (f32[4,32]{1,0:T(4,128)S(1)}, f32[4,32]{1,0:T(4,128)S(1)}, u32[]{:S(2)}, u32[]{:S(2)}) collective-permute-start(f32[4,32]{1,0:T(4,128)S(1)} %slice.126), channel_id=1, source_target_pairs={{0,1},{1,0},{2,3},{3,2},{4,5},{5,4},{6,7},{7,6},{8,9},{9,8},{10,11... | collective-permute-start | bytes 1544 | tf_op jit(solution)/shard_map/ppermute | solution.py:179

commit v4 on v3

v4 whole, which is shorter than its diff:
```python
import functools

import jax
import jax.numpy as jnp
from jax import lax
from jax.experimental import pallas as pl
from jax.experimental.pallas import tpu as pltpu
from jax.sharding import PartitionSpec as P

LANES = 128
LOWEST = -1e30
IN_VMEM = pl.BlockSpec(memory_space=pltpu.VMEM)
ANYWHERE = pl.BlockSpec(memory_space=pl.ANY)


def normalise(values, gain):
    values = values.astype(jnp.float32)
    squares = jnp.mean(values * values, axis=1, keepdims=True)
    return values * lax.rsqrt(squares + 1e-06) * gain


def norm_kernel(hidden_hbm, gain_hbm, count, out_ref, live_ref, hidden, gain, sems):
    copies = [
        pltpu.make_async_copy(source, target, sems.at[number])
        for number, (source, target) in enumerate(((hidden_hbm, hidden), (gain_hbm, gain)))
    ]
    for copy in copies:
        copy.start()
    for copy in copies:
        copy.wait()
    row = lax.broadcasted_iota(jnp.int32, hidden.shape, 0)
    alive = row < jnp.broadcast_to(count[...], hidden.shape)
    out_ref[...] = jnp.where(alive, normalise(hidden[...], gain[...]), 0.0).astype(jnp.bfloat16)
    column = lax.broadcasted_iota(jnp.int32, live_ref.shape, 1)
    live_ref[...] = (column < jnp.broadcast_to(count[...], live_ref.shape)).astype(jnp.float32)


def norm_rows(hidden_rows, gain, live_count):
    args = (hidden_rows, gain, live_count)
    return pl.pallas_call(
        norm_kernel,
        in_specs=[ANYWHERE, ANYWHERE, IN_VMEM],
        out_specs=[IN_VMEM] * 2,
        out_shape=[
            jax.ShapeDtypeStruct(hidden_rows.shape, jnp.bfloat16),
            jax.ShapeDtypeStruct((1, hidden_rows.shape[0]), jnp.float32),
        ],
        scratch_shapes=[pltpu.VMEM(x.shape, x.dtype) for x in args[:2]] + [pltpu.SemaphoreType.DMA((2,))],
        compiler_params=pltpu.CompilerParams(vmem_limit_bytes=3 * 2**20),
        cost_estimate=pl.CostEstimate(flops=10**11, bytes_accessed=10**8, transcendentals=0),
    )(*(pltpu.with_memory_space_constraint(x, pltpu.HBM) for x in args[:2]), live_count)


def column_of(tokens):
    wide = jnp.broadcast_to(tokens.astype(jnp.float32), (LANES, tokens.shape[1]))
    return wide.T.astype(jnp.int32)


def sweep(n_tiles, multiply, collect):
    multiply(0, 0)
    pairs = (n_tiles - 1) // 2

    @pl.loop(0, pairs)
    def _(pair):
        tile = pair * 2
        multiply(tile + 1, 1)
        collect(tile, 0)
        multiply(tile + 2, 0)
        collect(tile + 1, 1)

    if n_tiles % 2:
        collect(n_tiles - 1, 0)
    else:
        multiply(n_tiles - 1, 1)
        collect(n_tiles - 2, 0)
        collect(n_tiles - 1, 1)


def head_kernel(tile, counts, *refs):
    n_blocks = len(refs) - 14
    blocks, refs = refs[:n_blocks], refs[n_blocks:]
    token_ref, head, kept_ref, sent_ref, rows, packed, chosen, logits, wanted, by_row = refs[:10]
    top, total, spread, picked = refs[10:]
    own, depth = blocks[0].shape
    width = head.shape[1]
    me = lax.axis_index("vocab")
    n_rows = n_blocks * own

    by_row[...] = column_of(token_ref[...])
    lane = lax.broadcasted_iota(jnp.int32, (own, LANES), 1)
    for number, block in enumerate(blocks):
        place = slice(number * own, (number + 1) * own)
        values = block[...]
        rows[place, :depth] = values
        pieces = [jnp.abs(values[:, c : c + LANES]) for c in range(0, depth, LANES)]
        largest = functools.reduce(jnp.maximum, pieces).astype(jnp.float32)
        filled = jnp.max(largest, axis=1, keepdims=True) > 0.0
        spread[place, :] = jnp.broadcast_to(jnp.where(filled, 1.0, 0.0), (own, LANES))
        token = by_row[pl.ds(pl.multiple_of(lax.bitwise_xor(me, number) * own, own), own), :]
        digits = jnp.where(
            lane == 0, token // 4096, jnp.where(lane == 1, token // 64 % 64, token % 64)
        )
        rows[place, depth:] = jnp.where(lane < 3, digits, 0).astype(jnp.float32).astype(jnp.bfloat16)

    filled = spread[...]
    row = lax.broadcasted_iota(jnp.int32, (n_rows, n_rows), 0)
    column = lax.broadcasted_iota(jnp.int32, (n_rows, n_rows), 1)
    earlier = (column < row).astype(jnp.float32).astype(jnp.bfloat16)
    position = jnp.dot(earlier, filled.astype(jnp.bfloat16), preferred_element_type=jnp.float32)
    n_filled = jnp.max(position + filled).astype(jnp.int32)
    position = jnp.where(filled > 0.0, position, -1.0).astype(jnp.int32)
    lane = lax.broadcasted_iota(jnp.int32, (n_rows, LANES), 1)
    for first in range(0, n_rows, LANES):
        hit = (position == lane + first).astype(jnp.float32)
        chosen[:, first : first + LANES] = hit.astype(jnp.bfloat16)
    across = (((0,), (0,)), ((), ()))
    for first in range(0, depth, 512):
        piece = slice(first, first + 512)
        packed[:, piece] = lax.dot_general(
            chosen[...], rows[:, piece], across, preferred_element_type=jnp.float32
        ).astype(jnp.bfloat16)
    digits = lax.dot_general(chosen[...], rows[:, depth:], across, preferred_element_type=jnp.float32)
    token = (digits[:, 0:1] * 4096.0 + digits[:, 1:2] * 64.0 + digits[:, 2:3]).astype(jnp.int32)
    wanted[...] = token - me * width - lane
    top[...] = jnp.full(top.shape, LOWEST, jnp.float32)
    for sums in (total, spread, picked):
        sums[...] = jnp.zeros(sums.shape, jnp.float32)

    def work(count):
        def multiply(index, slot):
            columns = pl.ds(pl.multiple_of(index * tile, tile), tile)
            logits[slot, :count] = jnp.dot(
                packed[:count, :], head[:, columns], preferred_element_type=jnp.float32
            )

        def collect(index, slot):
            step = 32
            for begin in range(0, count, step):
                place = slice(begin, min(begin + step, count))
                pieces = [logits[slot, place, c : c + LANES] for c in range(0, tile, LANES)]
                last = top[place]
                new = jnp.maximum(last, functools.reduce(jnp.maximum, pieces))
                shift = last - new
                factor = jnp.exp(shift)
                sums = total[place]
                spreads = (spread[place] + shift * sums) * factor
                sums = sums * factor
                found = picked[place]
                target = wanted[place]
                for number, piece in enumerate(pieces):
                    shifted = piece - new
                    power = jnp.exp(shifted)
                    sums = sums + power
                    spreads = spreads + power * shifted
                    found = jnp.where(target == index * tile + number * LANES, piece, found)
                top[place] = new
                total[place] = sums
                spread[place] = spreads
                picked[place] = found

        sweep(width // tile, multiply, collect)

    for fewer, count in zip((0,) + counts, counts):

        @pl.when((n_filled > fewer) & (n_filled <= count))
        def _():
            work(count)

    row_top = jnp.max(top[...], axis=1, keepdims=True)
    shift = top[...] - row_top
    factor = jnp.exp(shift)
    row_total = jnp.sum(total[...] * factor, axis=1, keepdims=True)
    row_spread = jnp.sum((spread[...] + shift * total[...]) * factor, axis=1, keepdims=True)
    row_picked = jnp.sum(picked[...], axis=1, keepdims=True)
    kind = lane % 4
    values = jnp.where(
        kind == 0,
        row_top,
        jnp.where(kind == 1, row_total, jnp.where(kind == 2, row_spread, row_picked)),
    )
    high = values.astype(jnp.bfloat16)
    rest = values - high.astype(jnp.float32)
    middle = rest.astype(jnp.bfloat16)
    low = (rest - middle.astype(jnp.float32)).astype(jnp.bfloat16)
    parts = jnp.where(
        lane < 4,
        high.astype(jnp.float32),
        jnp.where(lane < 8, middle.astype(jnp.float32), low.astype(jnp.float32)),
    ).astype(jnp.bfloat16)
    unpacked = jnp.dot(chosen[...], parts, preferred_element_type=jnp.float32)
    table = jnp.where(lane == 12, filled, unpacked).T
    sums = table[0:4] + table[4:8] + table[8:12]
    known = jnp.where(lax.broadcasted_iota(jnp.int32, sums.shape, 0) == 1, float(width), 0.0)
    sums = sums + known * (1.0 - table[12:13])
    kept_ref[...] = sums[:, : n_rows // 2]
    sent_ref[...] = sums[:, n_rows // 2 :]


def head_stats(blocks, tokens, head):
    own, depth = blocks[0].shape
    width = head.shape[1]
    tile = next(t for t in (1024, 1280, 512, 256, 128) if width % t == 0)
    n_rows = own * len(blocks)
    counts = tuple(n_rows * k // 8 for k in (4, 5, 6, 7, 8))
    args = [*blocks, tokens, pltpu.with_memory_space_constraint(head, pltpu.VMEM)]
    lanes = pltpu.VMEM((n_rows, LANES), jnp.float32)
    return pl.pallas_call(
        functools.partial(head_kernel, tile, counts),
        in_specs=[IN_VMEM] * len(args),
        out_specs=[IN_VMEM] * 2,
        out_shape=[jax.ShapeDtypeStruct((4, n_rows // 2), jnp.float32)] * 2,
        scratch_shapes=[
            pltpu.VMEM((n_rows, depth + LANES), jnp.bfloat16),
            pltpu.VMEM((n_rows, depth), jnp.bfloat16),
            pltpu.VMEM((n_rows, n_rows), jnp.bfloat16),
            pltpu.VMEM((2, n_rows, tile), jnp.float32),
            pltpu.VMEM((n_rows, LANES), jnp.int32),
            pltpu.VMEM((n_rows, LANES), jnp.int32),
            *[lanes] * 4,
        ],
        compiler_params=pltpu.CompilerParams(
            vmem_limit_bytes=n_rows * (6 * depth + 8 * tile + 8 * n_rows + 64 * LANES) + 2**22
        ),
        cost_estimate=pl.CostEstimate(flops=1, bytes_accessed=500 * 2**20, transcendentals=0),
    )(*args)


def merge(mine, theirs):
    top = jnp.maximum(mine[0], theirs[0])
    a, b = mine[0] - top, theirs[0] - top
    fa, fb = jnp.exp(a), jnp.exp(b)
    total = mine[1] * fa + theirs[1] * fb
    spread = (mine[2] + a * mine[1]) * fa + (theirs[2] + b * theirs[1]) * fb
    return jnp.stack([top, total, spread, mine[3] + theirs[3]])


def swap(array, distance, size):
    return lax.ppermute(array, "vocab", [(i, i ^ distance) for i in range(size)])


def gather(normed, size):
    blocks = {0: normed}
    for d in sorted(range(1, size), key=lambda d: (bin(d).count("1"), -d)):
        distance = d & -d if d % 4 != 3 or d < 4 else 2
        if d == size // 2 + size // 4:
            direct = [1 << k for k in range(size.bit_length() - 1)]
            for k, block in zip(direct, lax.optimization_barrier(tuple(blocks[k] for k in direct))):
                blocks[k] = block
        blocks[d] = swap(blocks[d ^ distance], distance, size)
    return [blocks[d] for d in range(size)]


def per_device(size, hidden_rows, norm_gain, head_weight, token_ids, live_count):
    own = hidden_rows.shape[0]
    tokens = token_ids[None, :]
    normed, live = norm_rows(hidden_rows, norm_gain[None, :], live_count[None, :])
    kept, sent = head_stats(gather(normed, size), tokens, head_weight)
    distance = size // 2
    while True:
        stats = merge(kept, swap(sent, distance, size))
        distance //= 2
        if not distance:
            break
        kept, sent = stats[:, : distance * own], stats[:, distance * own :]
    top, total, spread, picked = lax.optimization_barrier(tuple(stats))
    log_total = jnp.log(total)
    logprob = picked - top - log_total
    entropy = log_total - spread / total
    live = live[0] > 0.0
    return jnp.where(live, logprob, 0.0), jnp.where(live, entropy, 0.0)


def solution(mesh):
    placed = (P(("req", "vocab"), None), P(), P(None, "vocab"), P("req"), P(("req", "vocab")))
    return jax.shard_map(
        functools.partial(per_device, mesh.shape["vocab"]),
        mesh=mesh,
        in_specs=placed,
        out_specs=(P(("req", "vocab")), P(("req", "vocab"))),
        check_vma=False,
    )
```

time: 51.2 us -> 46.6 us (0.910)
  Pallas kernels: 14.9 us -> 10.9 us
  starting transfers between devices: 14.7 us -> 16.4 us
  waiting for transfers between devices: 18.8 us -> 17.1 us
    pallas_call x2, Pallas kernels: 14.9 us -> 10.9 us  [the longest x1 9.66 us: head_stats(): pl.pallas_call(functools.partial(head_kernel, tile, counts), in_specs=[IN...]
    ppermute x10, waiting for transfers between devices: 18.8 us -> 17.1 us  [swap(): lax.ppermute(array, 'vocab', [(i, i ^ distance) for i in range(size)])]
    ppermute x10, starting transfers between devices: 14.7 us -> 16.4 us  [swap(): lax.ppermute(array, 'vocab', [(i, i ^ distance) for i in range(size)])]
    select_n x2 -> x1, other arithmetic: 1.05 us -> 0.53 us  [per_device(): return (jnp.where(live, logprob, 0.0), jnp.where(live, entropy, 0.0))]
  transfers between devices with their start and end apart: 10 -> 10, of which waited for: 7 -> 8; matrix products, arithmetic and copies ran while one was open for 0% -> 0% of each run, Pallas kernels for 0% -> 0%
where the time goes in v4:
time: 46.6 us; the launch traced here: 46.4 us
  waiting for transfers between devices  17.1 us (37%)
  starting transfers between devices  16.4 us (35%)
  Pallas kernels  10.9 us (23%)
  between operations  1.35 us (3%)
  other arithmetic  0.62 us (1%)
    ppermute x10, waiting for transfers between devices, swap(): lax.ppermute(array, 'vocab', [(i, i ^ distance) for i in range(size)])  17.1 us
    ppermute x10, starting transfers between devices, swap(): lax.ppermute(array, 'vocab', [(i, i ^ distance) for i in range(size)])  16.4 us
    pallas_call x1, Pallas kernels, head_stats(): pl.pallas_call(functools.partial(head_kernel, tile, counts), in_specs=[IN...  9.66 us
    pallas_call x1, Pallas kernels, norm_rows(): pl.pallas_call(norm_kernel, in_specs=[ANYWHERE, ANYWHERE, IN_VMEM], out_s...  1.21 us
  transfers between devices with their start and end apart: 10, of which 8 were waited for; matrix products, arithmetic and copies ran while one was open for 0% of the time, Pallas kernels for 0%

profile of v4, /device:TPU:0, one launch (start us, length us, event | category | flops | bytes accessed | tf_op | source)
XLA Modules:
  0.0 46.4 jit_solution(12454250452907457371)
XLA Ops:
  1.3 0.0 copy-start
  1.3 0.0 copy-start.1
  1.3 1.2 %shard_map.68 = (bf16[32,2048]{1,0:T(8,128)(2,1)S(1)}, f32[1,32]{1,0:T(1,128)S(1)}) custom-call(bf16[32,2048]{1,0:T(8,128)(2,1)} %hidden_hbm.1, f32[1,2048]{1,0:T(1,128)} %bitcast.52, s32[1,1]{1,0:T(1,128)} %bitcast.50.count), custom_call_target="tpu_custom_call" | custom-call | flops 99999997952 | bytes 100000000 | tf_op jit(solution)/shard_map/pallas_call | solution.py:40
  2.5 4.1 %collective-permute-start.2 = (bf16[32,2048]{1,0:T(8,128)(2,1)S(1)}, bf16[32,2048]{1,0:T(8,128)(2,1)S(1)}, u32[]{:S(2)}, u32[]{:S(2)}) collective-permute-start(bf16[32,2048]{1,0:T(8,128)(2,1)S(1)} %get-tuple-element.14.refs_0_), channel_id=1, source_target_pairs={{0,4},{1,5},{2,6},{3,7},{4,0},{5,1},{6,2},{7,3},{8,12},{9,13},{10,... | collective-permute-start | bytes 393224 | tf_op jit(solution)/shard_map/ppermute | solution.py:238
  6.6 1.6 %collective-permute-start.1 = (bf16[32,2048]{1,0:T(8,128)(2,1)S(1)}, bf16[32,2048]{1,0:T(8,128)(2,1)S(1)}, u32[]{:S(2)}, u32[]{:S(2)}) collective-permute-start(bf16[32,2048]{1,0:T(8,128)(2,1)S(1)} %get-tuple-element.14.refs_0_), channel_id=1, source_target_pairs={{0,2},{1,3},{2,0},{3,1},{4,6},{5,7},{6,4},{7,5},{8,10},{9,11},{10,... | collective-permute-start | bytes 393224 | tf_op jit(solution)/shard_map/ppermute | solution.py:238
  8.2 1.5 %collective-permute-start = (bf16[32,2048]{1,0:T(8,128)(2,1)S(1)}, bf16[32,2048]{1,0:T(8,128)(2,1)S(1)}, u32[]{:S(2)}, u32[]{:S(2)}) collective-permute-start(bf16[32,2048]{1,0:T(8,128)(2,1)S(1)} %get-tuple-element.14.refs_0_), channel_id=1, source_target_pairs={{0,1},{1,0},{2,3},{3,2},{4,5},{5,4},{6,7},{7,6},{8,9},{9,8},{10,11... | collective-permute-start | bytes 393224 | tf_op jit(solution)/shard_map/ppermute | solution.py:238
  9.7 3.3 %collective-permute-done.2.refs_4_ = bf16[32,2048]{1,0:T(8,128)(2,1)S(1)} collective-permute-done((bf16[32,2048]{1,0:T(8,128)(2,1)S(1)}, bf16[32,2048]{1,0:T(8,128)(2,1)S(1)}, u32[]{:S(2)}, u32[]{:S(2)}) %collective-permute-start.2) | collective-permute-done | bytes 131104 | tf_op jit(solution)/shard_map/ppermute | solution.py:238
  13.0 0.2 collective-permute-done.1.refs_2_
  13.2 0.0 collective-permute-done.refs_1_
  13.2 1.6 %collective-permute-start.4 = (bf16[32,2048]{1,0:T(8,128)(2,1)S(1)}, bf16[32,2048]{1,0:T(8,128)(2,1)S(1)}, u32[]{:S(2)}, u32[]{:S(2)}) collective-permute-start(bf16[32,2048]{1,0:T(8,128)(2,1)S(1)} %collective-permute-done.2.refs_4_), channel_id=1, source_target_pairs={{0,1},{1,0},{2,3},{3,2},{4,5},{5,4},{6,7},{7,6},{8,9},{9,8},{10,11... | collective-permute-start | bytes 393224 | tf_op jit(solution)/shard_map/ppermute | solution.py:238
  14.8 1.4 %collective-permute-start.5 = (bf16[32,2048]{1,0:T(8,128)(2,1)S(1)}, bf16[32,2048]{1,0:T(8,128)(2,1)S(1)}, u32[]{:S(2)}, u32[]{:S(2)}) collective-permute-start(bf16[32,2048]{1,0:T(8,128)(2,1)S(1)} %collective-permute-done.2.refs_4_), channel_id=1, source_target_pairs={{0,2},{1,3},{2,0},{3,1},{4,6},{5,7},{6,4},{7,5},{8,10},{9,11},{10,... | collective-permute-start | bytes 393224 | tf_op jit(solution)/shard_map/ppermute | solution.py:238
  16.2 0.5 %collective-permute-start.3 = (bf16[32,2048]{1,0:T(8,128)(2,1)S(1)}, bf16[32,2048]{1,0:T(8,128)(2,1)S(1)}, u32[]{:S(2)}, u32[]{:S(2)}) collective-permute-start(bf16[32,2048]{1,0:T(8,128)(2,1)S(1)} %collective-permute-done.1.refs_2_), channel_id=1, source_target_pairs={{0,1},{1,0},{2,3},{3,2},{4,5},{5,4},{6,7},{7,6},{8,9},{9,8},{10,11... | collective-permute-start | bytes 393224 | tf_op jit(solution)/shard_map/ppermute | solution.py:238
  16.7 2.6 %collective-permute-done.4.refs_5_ = bf16[32,2048]{1,0:T(8,128)(2,1)S(1)} collective-permute-done((bf16[32,2048]{1,0:T(8,128)(2,1)S(1)}, bf16[32,2048]{1,0:T(8,128)(2,1)S(1)}, u32[]{:S(2)}, u32[]{:S(2)}) %collective-permute-start.4) | collective-permute-done | bytes 131104 | tf_op jit(solution)/shard_map/ppermute | solution.py:238
  19.3 1.2 %collective-permute-start.6 = (bf16[32,2048]{1,0:T(8,128)(2,1)S(1)}, bf16[32,2048]{1,0:T(8,128)(2,1)S(1)}, u32[]{:S(2)}, u32[]{:S(2)}) collective-permute-start(bf16[32,2048]{1,0:T(8,128)(2,1)S(1)} %collective-permute-done.4.refs_5_), channel_id=1, source_target_pairs={{0,2},{1,3},{2,0},{3,1},{4,6},{5,7},{6,4},{7,5},{8,10},{9,11},{10,... | collective-permute-start | bytes 393224 | tf_op jit(solution)/shard_map/ppermute | solution.py:238
  20.5 0.7 %collective-permute-done.3.refs_3_ = bf16[32,2048]{1,0:T(8,128)(2,1)S(1)} collective-permute-done((bf16[32,2048]{1,0:T(8,128)(2,1)S(1)}, bf16[32,2048]{1,0:T(8,128)(2,1)S(1)}, u32[]{:S(2)}, u32[]{:S(2)}) %collective-permute-start.3) | collective-permute-done | bytes 131104 | tf_op jit(solution)/shard_map/ppermute | solution.py:238
  21.1 0.0 collective-permute-done.5.refs_6_
  21.1 3.1 %collective-permute-done.6.refs_7_ = bf16[32,2048]{1,0:T(8,128)(2,1)S(1)} collective-permute-done((bf16[32,2048]{1,0:T(8,128)(2,1)S(1)}, bf16[32,2048]{1,0:T(8,128)(2,1)S(1)}, u32[]{:S(2)}, u32[]{:S(2)}) %collective-permute-start.6) | collective-permute-done | bytes 131104 | tf_op jit(solution)/shard_map/ppermute | solution.py:238
  24.3 0.0 copy-done
  24.3 0.0 copy-done.1
  24.3 9.7 %shard_map.69 = (f32[4,128]{1,0:T(4,128)S(1)}, f32[4,128]{1,0:T(4,128)S(1)}) custom-call(bf16[32,2048]{1,0:T(8,128)(2,1)S(1)} %get-tuple-element.14.refs_0_, bf16[32,2048]{1,0:T(8,128)(2,1)S(1)} %collective-permute-done.refs_1_, bf16[32,2048]{1,0:T(8,128)(2,1)S(1)} %collective-permute-done.1.refs_2_, bf16[32,2048]{1,0:T(8,128)(2,1)S(1)} %collective-permute-done.3.refs_3_, ...), custom_call_target="tpu_custom_call" | custom-call | flops 1 | bytes 524288000 | tf_op jit(solution)/shard_map/pallas_call | solution.py:207
  33.9 2.1 %collective-permute-start.7 = (f32[4,128]{1,0:T(4,128)S(1)}, f32[4,128]{1,0:T(4,128)S(1)}, u32[]{:S(2)}, u32[]{:S(2)}) collective-permute-start(f32[4,128]{1,0:T(4,128)S(1)} %get-tuple-element.19), channel_id=1, source_target_pairs={{0,4},{1,5},{2,6},{3,7},{4,0},{5,1},{6,2},{7,3},{8,12},{9,13},{10,... | collective-permute-start | bytes 6152 | tf_op jit(solution)/shard_map/ppermute | solution.py:238
  36.0 2.4 %collective-permute-done.7 = f32[4,128]{1,0:T(4,128)S(1)} collective-permute-done((f32[4,128]{1,0:T(4,128)S(1)}, f32[4,128]{1,0:T(4,128)S(1)}, u32[]{:S(2)}, u32[]{:S(2)}) %collective-permute-start.7) | collective-permute-done | bytes 2080 | tf_op jit(solution)/shard_map/ppermute | solution.py:238
  38.5 0.1 slice.117
  38.6 1.2 %collective-permute-start.8 = (f32[4,64]{1,0:T(4,128)S(1)}, f32[4,64]{1,0:T(4,128)S(1)}, u32[]{:S(2)}, u32[]{:S(2)}) collective-permute-start(f32[4,64]{1,0:T(4,128)S(1)} %slice.117), channel_id=1, source_target_pairs={{0,2},{1,3},{2,0},{3,1},{4,6},{5,7},{6,4},{7,5},{8,10},{9,11},{10,... | collective-permute-start | bytes 3080 | tf_op jit(solution)/shard_map/ppermute | solution.py:238
  39.8 2.4 %collective-permute-done.8 = f32[4,64]{1,0:T(4,128)S(1)} collective-permute-done((f32[4,64]{1,0:T(4,128)S(1)}, f32[4,64]{1,0:T(4,128)S(1)}, u32[]{:S(2)}, u32[]{:S(2)}) %collective-permute-start.8) | collective-permute-done | bytes 1056 | tf_op jit(solution)/shard_map/ppermute | solution.py:238
  42.2 0.1 slice.126
  42.3 1.3 %collective-permute-start.9 = (f32[4,32]{1,0:T(4,128)S(1)}, f32[4,32]{1,0:T(4,128)S(1)}, u32[]{:S(2)}, u32[]{:S(2)}) collective-permute-start(f32[4,32]{1,0:T(4,128)S(1)} %slice.126), channel_id=1, source_target_pairs={{0,1},{1,0},{2,3},{3,2},{4,5},{5,4},{6,7},{7,6},{8,9},{9,8},{10,11... | collective-permute-start | bytes 1544 | tf_op jit(solution)/shard_map/ppermute | solution.py:238
  43.6 2.3 %collective-permute-done.9 = f32[4,32]{1,0:T(4,128)S(1)} collective-permute-done((f32[4,32]{1,0:T(4,128)S(1)}, f32[4,32]{1,0:T(4,128)S(1)}, u32[]{:S(2)}, u32[]{:S(2)}) %collective-permute-start.9) | collective-permute-done | bytes 544 | tf_op jit(solution)/shard_map/ppermute | solution.py:238
  45.9 0.5 %bitcast_select_fusion = (f32[32]{0:T(128)}, f32[32]{0:T(128)}) fusion(f32[1,32]{1,0:T(1,128)S(1)} %get-tuple-element.13, f32[32]{0:T(128)S(1)} %get-tuple-element.23, f32[32]{0:T(128)S(1)} %fusion.3, f32[32]{0:T(128)S(1)} %add_bitcast_fusion, f32[32]{0:T(128)S(1)} %get-tuple-element.21), kind=kLoop, calls=%fused_computation.2 | loop fusion | flops 224 | bytes 896 | tf_op jit(solution)/shard_map/jit(_where)/select_n | solution.py:270
  (9 shorter events, 0.1 us)
Async XLA Ops:
  1.3 23.0 %copy-start = (bf16[2048,10240]{1,0:T(8,128)(2,1)S(1)}, bf16[2048,10240]{1,0:T(8,128)(2,1)}, u32[]{:S(2)}) copy-start(bf16[2048,10240]{1,0:T(8,128)(2,1)} %refs_9_.1) | copy-start | bytes 125829120
  1.3 23.0 %copy-start.1 = (s32[256]{0:T(256)S(1)}, s32[256]{0:T(256)}, u32[]{:S(2)}) copy-start(s32[256]{0:T(256)} %param.8) | copy-start | bytes 3076
  2.5 10.5 %collective-permute-start.2 = (bf16[32,2048]{1,0:T(8,128)(2,1)S(1)}, bf16[32,2048]{1,0:T(8,128)(2,1)S(1)}, u32[]{:S(2)}, u32[]{:S(2)}) collective-permute-start(bf16[32,2048]{1,0:T(8,128)(2,1)S(1)} %get-tuple-element.14.refs_0_), channel_id=1, source_target_pairs={{0,4},{1,5},{2,6},{3,7},{4,0},{5,1},{6,2},{7,3},{8,12},{9,13},{10,... | collective-permute-start | bytes 393224 | tf_op jit(solution)/shard_map/ppermute | solution.py:238
  6.6 6.6 %collective-permute-start.1 = (bf16[32,2048]{1,0:T(8,128)(2,1)S(1)}, bf16[32,2048]{1,0:T(8,128)(2,1)S(1)}, u32[]{:S(2)}, u32[]{:S(2)}) collective-permute-start(bf16[32,2048]{1,0:T(8,128)(2,1)S(1)} %get-tuple-element.14.refs_0_), channel_id=1, source_target_pairs={{0,2},{1,3},{2,0},{3,1},{4,6},{5,7},{6,4},{7,5},{8,10},{9,11},{10,... | collective-permute-start | bytes 393224 | tf_op jit(solution)/shard_map/ppermute | solution.py:238
  8.2 5.0 %collective-permute-start = (bf16[32,2048]{1,0:T(8,128)(2,1)S(1)}, bf16[32,2048]{1,0:T(8,128)(2,1)S(1)}, u32[]{:S(2)}, u32[]{:S(2)}) collective-permute-start(bf16[32,2048]{1,0:T(8,128)(2,1)S(1)} %get-tuple-element.14.refs_0_), channel_id=1, source_target_pairs={{0,1},{1,0},{2,3},{3,2},{4,5},{5,4},{6,7},{7,6},{8,9},{9,8},{10,11... | collective-permute-start | bytes 393224 | tf_op jit(solution)/shard_map/ppermute | solution.py:238
  13.2 6.1 %collective-permute-start.4 = (bf16[32,2048]{1,0:T(8,128)(2,1)S(1)}, bf16[32,2048]{1,0:T(8,128)(2,1)S(1)}, u32[]{:S(2)}, u32[]{:S(2)}) collective-permute-start(bf16[32,2048]{1,0:T(8,128)(2,1)S(1)} %collective-permute-done.2.refs_4_), channel_id=1, source_target_pairs={{0,1},{1,0},{2,3},{3,2},{4,5},{5,4},{6,7},{7,6},{8,9},{9,8},{10,11... | collective-permute-start | bytes 393224 | tf_op jit(solution)/shard_map/ppermute | solution.py:238
  14.8 6.3 %collective-permute-start.5 = (bf16[32,2048]{1,0:T(8,128)(2,1)S(1)}, bf16[32,2048]{1,0:T(8,128)(2,1)S(1)}, u32[]{:S(2)}, u32[]{:S(2)}) collective-permute-start(bf16[32,2048]{1,0:T(8,128)(2,1)S(1)} %collective-permute-done.2.refs_4_), channel_id=1, source_target_pairs={{0,2},{1,3},{2,0},{3,1},{4,6},{5,7},{6,4},{7,5},{8,10},{9,11},{10,... | collective-permute-start | bytes 393224 | tf_op jit(solution)/shard_map/ppermute | solution.py:238
  16.2 5.0 %collective-permute-start.3 = (bf16[32,2048]{1,0:T(8,128)(2,1)S(1)}, bf16[32,2048]{1,0:T(8,128)(2,1)S(1)}, u32[]{:S(2)}, u32[]{:S(2)}) collective-permute-start(bf16[32,2048]{1,0:T(8,128)(2,1)S(1)} %collective-permute-done.1.refs_2_), channel_id=1, source_target_pairs={{0,1},{1,0},{2,3},{3,2},{4,5},{5,4},{6,7},{7,6},{8,9},{9,8},{10,11... | collective-permute-start | bytes 393224 | tf_op jit(solution)/shard_map/ppermute | solution.py:238
  19.3 5.0 %collective-permute-start.6 = (bf16[32,2048]{1,0:T(8,128)(2,1)S(1)}, bf16[32,2048]{1,0:T(8,128)(2,1)S(1)}, u32[]{:S(2)}, u32[]{:S(2)}) collective-permute-start(bf16[32,2048]{1,0:T(8,128)(2,1)S(1)} %collective-permute-done.4.refs_5_), channel_id=1, source_target_pairs={{0,2},{1,3},{2,0},{3,1},{4,6},{5,7},{6,4},{7,5},{8,10},{9,11},{10,... | collective-permute-start | bytes 393224 | tf_op jit(solution)/shard_map/ppermute | solution.py:238
  33.9 4.5 %collective-permute-start.7 = (f32[4,128]{1,0:T(4,128)S(1)}, f32[4,128]{1,0:T(4,128)S(1)}, u32[]{:S(2)}, u32[]{:S(2)}) collective-permute-start(f32[4,128]{1,0:T(4,128)S(1)} %get-tuple-element.19), channel_id=1, source_target_pairs={{0,4},{1,5},{2,6},{3,7},{4,0},{5,1},{6,2},{7,3},{8,12},{9,13},{10,... | collective-permute-start | bytes 6152 | tf_op jit(solution)/shard_map/ppermute | solution.py:238
  38.6 3.6 %collective-permute-start.8 = (f32[4,64]{1,0:T(4,128)S(1)}, f32[4,64]{1,0:T(4,128)S(1)}, u32[]{:S(2)}, u32[]{:S(2)}) collective-permute-start(f32[4,64]{1,0:T(4,128)S(1)} %slice.117), channel_id=1, source_target_pairs={{0,2},{1,3},{2,0},{3,1},{4,6},{5,7},{6,4},{7,5},{8,10},{9,11},{10,... | collective-permute-start | bytes 3080 | tf_op jit(solution)/shard_map/ppermute | solution.py:238
  42.3 3.6 %collective-permute-start.9 = (f32[4,32]{1,0:T(4,128)S(1)}, f32[4,32]{1,0:T(4,128)S(1)}, u32[]{:S(2)}, u32[]{:S(2)}) collective-permute-start(f32[4,32]{1,0:T(4,128)S(1)} %slice.126), channel_id=1, source_target_pairs={{0,1},{1,0},{2,3},{3,2},{4,5},{5,4},{6,7},{7,6},{8,9},{9,8},{10,11... | collective-permute-start | bytes 1544 | tf_op jit(solution)/shard_map/ppermute | solution.py:238

commit v5 on v4

--- a/solution.py
+++ b/solution.py
@@ -60,7 +60,7 @@
     multiply(0, 0)
     pairs = (n_tiles - 1) // 2
 
-    @pl.loop(0, pairs)
+    @pl.loop(0, pairs, unroll=4 if pairs % 4 == 0 else 1)
     def _(pair):
         tile = pair * 2
         multiply(tile + 1, 1)
@@ -98,7 +98,7 @@
         spread[place, :] = jnp.broadcast_to(jnp.where(filled, 1.0, 0.0), (own, LANES))
         token = by_row[pl.ds(pl.multiple_of(lax.bitwise_xor(me, number) * own, own), own), :]
         digits = jnp.where(
-            lane == 0, token // 4096, jnp.where(lane == 1, token // 64 % 64, token % 64)
+            lane == 0, token >> 12, jnp.where(lane == 1, (token >> 6) & 63, token & 63)
         )
         rows[place, depth:] = jnp.where(lane < 3, digits, 0).astype(jnp.float32).astype(jnp.bfloat16)
 
@@ -113,13 +113,14 @@
     for first in range(0, n_rows, LANES):
         hit = (position == lane + first).astype(jnp.float32)
         chosen[:, first : first + LANES] = hit.astype(jnp.bfloat16)
-    across = (((0,), (0,)), ((), ()))
+    spot = position.astype(jnp.float32).T[0:1, :].astype(jnp.int32)
+    packing = (row == jnp.broadcast_to(spot, row.shape)).astype(jnp.float32).astype(jnp.bfloat16)
     for first in range(0, depth, 512):
         piece = slice(first, first + 512)
-        packed[:, piece] = lax.dot_general(
-            chosen[...], rows[:, piece], across, preferred_element_type=jnp.float32
+        packed[:, piece] = jnp.dot(
+            packing, rows[:, piece], preferred_element_type=jnp.float32
         ).astype(jnp.bfloat16)
-    digits = lax.dot_general(chosen[...], rows[:, depth:], across, preferred_element_type=jnp.float32)
+    digits = jnp.dot(packing, rows[:, depth:], preferred_element_type=jnp.float32)
     token = (digits[:, 0:1] * 4096.0 + digits[:, 1:2] * 64.0 + digits[:, 2:3]).astype(jnp.int32)
     wanted[...] = token - me * width - lane
     top[...] = jnp.full(top.shape, LOWEST, jnp.float32)
@@ -201,7 +202,7 @@
     width = head.shape[1]
     tile = next(t for t in (1024, 1280, 512, 256, 128) if width % t == 0)
     n_rows = own * len(blocks)
-    counts = tuple(n_rows * k // 8 for k in (4, 5, 6, 7, 8))
+    counts = tuple(n_rows * k // 8 for k in (4, 5, 6, 8))
     args = [*blocks, tokens, pltpu.with_memory_space_constraint(head, pltpu.VMEM)]
     lanes = pltpu.VMEM((n_rows, LANES), jnp.float32)
     return pl.pallas_call(

time: 46.6 us -> 46.5 us (level); the launches traced: 46.4 us -> 47.1 us
  Pallas kernels: 10.9 us -> 11.6 us
    pallas_call x1, Pallas kernels: 9.66 us -> 10.4 us  [head_stats(): pl.pallas_call(functools.partial(head_kernel, tile, counts), in_specs=[IN...]
where the time goes in v5:
time: 46.5 us; the launch traced here: 47.1 us
  waiting for transfers between devices  17.1 us (37%)
  starting transfers between devices  16.4 us (35%)
  Pallas kernels  11.6 us (25%)
  between operations  1.35 us (3%)
  other arithmetic  0.62 us (1%)
    ppermute x10, waiting for transfers between devices, swap(): lax.ppermute(array, 'vocab', [(i, i ^ distance) for i in range(size)])  17.1 us
    ppermute x10, starting transfers between devices, swap(): lax.ppermute(array, 'vocab', [(i, i ^ distance) for i in range(size)])  16.4 us
    pallas_call x1, Pallas kernels, head_stats(): pl.pallas_call(functools.partial(head_kernel, tile, counts), in_specs=[IN...  10.4 us
    pallas_call x1, Pallas kernels, norm_rows(): pl.pallas_call(norm_kernel, in_specs=[ANYWHERE, ANYWHERE, IN_VMEM], out_s...  1.21 us
  transfers between devices with their start and end apart: 10, of which 8 were waited for; matrix products, arithmetic and copies ran while one was open for 0% of the time, Pallas kernels for 0%

profile of v5, /device:TPU:0, one launch (start us, length us, event | category | flops | bytes accessed | tf_op | source)
XLA Modules:
  0.0 47.1 jit_solution(2578490707764496209)
XLA Ops:
  1.3 0.0 copy-start
  1.3 0.0 copy-start.1
  1.3 1.2 %shard_map.68 = (bf16[32,2048]{1,0:T(8,128)(2,1)S(1)}, f32[1,32]{1,0:T(1,128)S(1)}) custom-call(bf16[32,2048]{1,0:T(8,128)(2,1)} %hidden_hbm.1, f32[1,2048]{1,0:T(1,128)} %bitcast.52, s32[1,1]{1,0:T(1,128)} %bitcast.50.count), custom_call_target="tpu_custom_call" | custom-call | flops 99999997952 | bytes 100000000 | tf_op jit(solution)/shard_map/pallas_call | solution.py:40
  2.5 4.1 %collective-permute-start.2 = (bf16[32,2048]{1,0:T(8,128)(2,1)S(1)}, bf16[32,2048]{1,0:T(8,128)(2,1)S(1)}, u32[]{:S(2)}, u32[]{:S(2)}) collective-permute-start(bf16[32,2048]{1,0:T(8,128)(2,1)S(1)} %get-tuple-element.14.refs_0_), channel_id=1, source_target_pairs={{0,4},{1,5},{2,6},{3,7},{4,0},{5,1},{6,2},{7,3},{8,12},{9,13},{10,... | collective-permute-start | bytes 393224 | tf_op jit(solution)/shard_map/ppermute | solution.py:239
  6.6 1.6 %collective-permute-start.1 = (bf16[32,2048]{1,0:T(8,128)(2,1)S(1)}, bf16[32,2048]{1,0:T(8,128)(2,1)S(1)}, u32[]{:S(2)}, u32[]{:S(2)}) collective-permute-start(bf16[32,2048]{1,0:T(8,128)(2,1)S(1)} %get-tuple-element.14.refs_0_), channel_id=1, source_target_pairs={{0,2},{1,3},{2,0},{3,1},{4,6},{5,7},{6,4},{7,5},{8,10},{9,11},{10,... | collective-permute-start | bytes 393224 | tf_op jit(solution)/shard_map/ppermute | solution.py:239
  8.2 1.5 %collective-permute-start = (bf16[32,2048]{1,0:T(8,128)(2,1)S(1)}, bf16[32,2048]{1,0:T(8,128)(2,1)S(1)}, u32[]{:S(2)}, u32[]{:S(2)}) collective-permute-start(bf16[32,2048]{1,0:T(8,128)(2,1)S(1)} %get-tuple-element.14.refs_0_), channel_id=1, source_target_pairs={{0,1},{1,0},{2,3},{3,2},{4,5},{5,4},{6,7},{7,6},{8,9},{9,8},{10,11... | collective-permute-start | bytes 393224 | tf_op jit(solution)/shard_map/ppermute | solution.py:239
  9.7 3.3 %collective-permute-done.2.refs_4_ = bf16[32,2048]{1,0:T(8,128)(2,1)S(1)} collective-permute-done((bf16[32,2048]{1,0:T(8,128)(2,1)S(1)}, bf16[32,2048]{1,0:T(8,128)(2,1)S(1)}, u32[]{:S(2)}, u32[]{:S(2)}) %collective-permute-start.2) | collective-permute-done | bytes 131104 | tf_op jit(solution)/shard_map/ppermute | solution.py:239
  13.0 0.2 collective-permute-done.1.refs_2_
  13.2 0.0 collective-permute-done.refs_1_
  13.2 1.6 %collective-permute-start.4 = (bf16[32,2048]{1,0:T(8,128)(2,1)S(1)}, bf16[32,2048]{1,0:T(8,128)(2,1)S(1)}, u32[]{:S(2)}, u32[]{:S(2)}) collective-permute-start(bf16[32,2048]{1,0:T(8,128)(2,1)S(1)} %collective-permute-done.2.refs_4_), channel_id=1, source_target_pairs={{0,1},{1,0},{2,3},{3,2},{4,5},{5,4},{6,7},{7,6},{8,9},{9,8},{10,11... | collective-permute-start | bytes 393224 | tf_op jit(solution)/shard_map/ppermute | solution.py:239
  14.8 1.4 %collective-permute-start.5 = (bf16[32,2048]{1,0:T(8,128)(2,1)S(1)}, bf16[32,2048]{1,0:T(8,128)(2,1)S(1)}, u32[]{:S(2)}, u32[]{:S(2)}) collective-permute-start(bf16[32,2048]{1,0:T(8,128)(2,1)S(1)} %collective-permute-done.2.refs_4_), channel_id=1, source_target_pairs={{0,2},{1,3},{2,0},{3,1},{4,6},{5,7},{6,4},{7,5},{8,10},{9,11},{10,... | collective-permute-start | bytes 393224 | tf_op jit(solution)/shard_map/ppermute | solution.py:239
  16.2 0.5 %collective-permute-start.3 = (bf16[32,2048]{1,0:T(8,128)(2,1)S(1)}, bf16[32,2048]{1,0:T(8,128)(2,1)S(1)}, u32[]{:S(2)}, u32[]{:S(2)}) collective-permute-start(bf16[32,2048]{1,0:T(8,128)(2,1)S(1)} %collective-permute-done.1.refs_2_), channel_id=1, source_target_pairs={{0,1},{1,0},{2,3},{3,2},{4,5},{5,4},{6,7},{7,6},{8,9},{9,8},{10,11... | collective-permute-start | bytes 393224 | tf_op jit(solution)/shard_map/ppermute | solution.py:239
  16.7 2.6 %collective-permute-done.4.refs_5_ = bf16[32,2048]{1,0:T(8,128)(2,1)S(1)} collective-permute-done((bf16[32,2048]{1,0:T(8,128)(2,1)S(1)}, bf16[32,2048]{1,0:T(8,128)(2,1)S(1)}, u32[]{:S(2)}, u32[]{:S(2)}) %collective-permute-start.4) | collective-permute-done | bytes 131104 | tf_op jit(solution)/shard_map/ppermute | solution.py:239
  19.3 1.2 %collective-permute-start.6 = (bf16[32,2048]{1,0:T(8,128)(2,1)S(1)}, bf16[32,2048]{1,0:T(8,128)(2,1)S(1)}, u32[]{:S(2)}, u32[]{:S(2)}) collective-permute-start(bf16[32,2048]{1,0:T(8,128)(2,1)S(1)} %collective-permute-done.4.refs_5_), channel_id=1, source_target_pairs={{0,2},{1,3},{2,0},{3,1},{4,6},{5,7},{6,4},{7,5},{8,10},{9,11},{10,... | collective-permute-start | bytes 393224 | tf_op jit(solution)/shard_map/ppermute | solution.py:239
  20.5 0.7 %collective-permute-done.3.refs_3_ = bf16[32,2048]{1,0:T(8,128)(2,1)S(1)} collective-permute-done((bf16[32,2048]{1,0:T(8,128)(2,1)S(1)}, bf16[32,2048]{1,0:T(8,128)(2,1)S(1)}, u32[]{:S(2)}, u32[]{:S(2)}) %collective-permute-start.3) | collective-permute-done | bytes 131104 | tf_op jit(solution)/shard_map/ppermute | solution.py:239
  21.1 0.0 collective-permute-done.5.refs_6_
  21.1 3.1 %collective-permute-done.6.refs_7_ = bf16[32,2048]{1,0:T(8,128)(2,1)S(1)} collective-permute-done((bf16[32,2048]{1,0:T(8,128)(2,1)S(1)}, bf16[32,2048]{1,0:T(8,128)(2,1)S(1)}, u32[]{:S(2)}, u32[]{:S(2)}) %collective-permute-start.6) | collective-permute-done | bytes 131104 | tf_op jit(solution)/shard_map/ppermute | solution.py:239
  24.3 0.0 copy-done
  24.3 0.0 copy-done.1
  24.3 10.4 %shard_map.69 = (f32[4,128]{1,0:T(4,128)S(1)}, f32[4,128]{1,0:T(4,128)S(1)}) custom-call(bf16[32,2048]{1,0:T(8,128)(2,1)S(1)} %get-tuple-element.14.refs_0_, bf16[32,2048]{1,0:T(8,128)(2,1)S(1)} %collective-permute-done.refs_1_, bf16[32,2048]{1,0:T(8,128)(2,1)S(1)} %collective-permute-done.1.refs_2_, bf16[32,2048]{1,0:T(8,128)(2,1)S(1)} %collective-permute-done.3.refs_3_, ...), custom_call_target="tpu_custom_call" | custom-call | flops 1 | bytes 524288000 | tf_op jit(solution)/shard_map/pallas_call | solution.py:208
  34.6 2.1 %collective-permute-start.7 = (f32[4,128]{1,0:T(4,128)S(1)}, f32[4,128]{1,0:T(4,128)S(1)}, u32[]{:S(2)}, u32[]{:S(2)}) collective-permute-start(f32[4,128]{1,0:T(4,128)S(1)} %get-tuple-element.19), channel_id=1, source_target_pairs={{0,4},{1,5},{2,6},{3,7},{4,0},{5,1},{6,2},{7,3},{8,12},{9,13},{10,... | collective-permute-start | bytes 6152 | tf_op jit(solution)/shard_map/ppermute | solution.py:239
  36.7 2.4 %collective-permute-done.7 = f32[4,128]{1,0:T(4,128)S(1)} collective-permute-done((f32[4,128]{1,0:T(4,128)S(1)}, f32[4,128]{1,0:T(4,128)S(1)}, u32[]{:S(2)}, u32[]{:S(2)}) %collective-permute-start.7) | collective-permute-done | bytes 2080 | tf_op jit(solution)/shard_map/ppermute | solution.py:239
  39.2 0.1 slice.117
  39.3 1.2 %collective-permute-start.8 = (f32[4,64]{1,0:T(4,128)S(1)}, f32[4,64]{1,0:T(4,128)S(1)}, u32[]{:S(2)}, u32[]{:S(2)}) collective-permute-start(f32[4,64]{1,0:T(4,128)S(1)} %slice.117), channel_id=1, source_target_pairs={{0,2},{1,3},{2,0},{3,1},{4,6},{5,7},{6,4},{7,5},{8,10},{9,11},{10,... | collective-permute-start | bytes 3080 | tf_op jit(solution)/shard_map/ppermute | solution.py:239
  40.5 2.4 %collective-permute-done.8 = f32[4,64]{1,0:T(4,128)S(1)} collective-permute-done((f32[4,64]{1,0:T(4,128)S(1)}, f32[4,64]{1,0:T(4,128)S(1)}, u32[]{:S(2)}, u32[]{:S(2)}) %collective-permute-start.8) | collective-permute-done | bytes 1056 | tf_op jit(solution)/shard_map/ppermute | solution.py:239
  42.9 0.1 slice.126
  43.0 1.3 %collective-permute-start.9 = (f32[4,32]{1,0:T(4,128)S(1)}, f32[4,32]{1,0:T(4,128)S(1)}, u32[]{:S(2)}, u32[]{:S(2)}) collective-permute-start(f32[4,32]{1,0:T(4,128)S(1)} %slice.126), channel_id=1, source_target_pairs={{0,1},{1,0},{2,3},{3,2},{4,5},{5,4},{6,7},{7,6},{8,9},{9,8},{10,11... | collective-permute-start | bytes 1544 | tf_op jit(solution)/shard_map/ppermute | solution.py:239
  44.2 2.3 %collective-permute-done.9 = f32[4,32]{1,0:T(4,128)S(1)} collective-permute-done((f32[4,32]{1,0:T(4,128)S(1)}, f32[4,32]{1,0:T(4,128)S(1)}, u32[]{:S(2)}, u32[]{:S(2)}) %collective-permute-start.9) | collective-permute-done | bytes 544 | tf_op jit(solution)/shard_map/ppermute | solution.py:239
  46.6 0.5 %bitcast_select_fusion = (f32[32]{0:T(128)}, f32[32]{0:T(128)}) fusion(f32[1,32]{1,0:T(1,128)S(1)} %get-tuple-element.13, f32[32]{0:T(128)S(1)} %get-tuple-element.23, f32[32]{0:T(128)S(1)} %fusion.3, f32[32]{0:T(128)S(1)} %add_bitcast_fusion, f32[32]{0:T(128)S(1)} %get-tuple-element.21), kind=kLoop, calls=%fused_computation.2 | loop fusion | flops 224 | bytes 896 | tf_op jit(solution)/shard_map/jit(_where)/select_n | solution.py:271
  (9 shorter events, 0.1 us)
Async XLA Ops:
  1.3 23.0 %copy-start = (bf16[2048,10240]{1,0:T(8,128)(2,1)S(1)}, bf16[2048,10240]{1,0:T(8,128)(2,1)}, u32[]{:S(2)}) copy-start(bf16[2048,10240]{1,0:T(8,128)(2,1)} %refs_9_.1) | copy-start | bytes 125829120
  1.3 23.0 %copy-start.1 = (s32[256]{0:T(256)S(1)}, s32[256]{0:T(256)}, u32[]{:S(2)}) copy-start(s32[256]{0:T(256)} %param.8) | copy-start | bytes 3076
  2.5 10.5 %collective-permute-start.2 = (bf16[32,2048]{1,0:T(8,128)(2,1)S(1)}, bf16[32,2048]{1,0:T(8,128)(2,1)S(1)}, u32[]{:S(2)}, u32[]{:S(2)}) collective-permute-start(bf16[32,2048]{1,0:T(8,128)(2,1)S(1)} %get-tuple-element.14.refs_0_), channel_id=1, source_target_pairs={{0,4},{1,5},{2,6},{3,7},{4,0},{5,1},{6,2},{7,3},{8,12},{9,13},{10,... | collective-permute-start | bytes 393224 | tf_op jit(solution)/shard_map/ppermute | solution.py:239
  6.6 6.6 %collective-permute-start.1 = (bf16[32,2048]{1,0:T(8,128)(2,1)S(1)}, bf16[32,2048]{1,0:T(8,128)(2,1)S(1)}, u32[]{:S(2)}, u32[]{:S(2)}) collective-permute-start(bf16[32,2048]{1,0:T(8,128)(2,1)S(1)} %get-tuple-element.14.refs_0_), channel_id=1, source_target_pairs={{0,2},{1,3},{2,0},{3,1},{4,6},{5,7},{6,4},{7,5},{8,10},{9,11},{10,... | collective-permute-start | bytes 393224 | tf_op jit(solution)/shard_map/ppermute | solution.py:239
  8.2 5.0 %collective-permute-start = (bf16[32,2048]{1,0:T(8,128)(2,1)S(1)}, bf16[32,2048]{1,0:T(8,128)(2,1)S(1)}, u32[]{:S(2)}, u32[]{:S(2)}) collective-permute-start(bf16[32,2048]{1,0:T(8,128)(2,1)S(1)} %get-tuple-element.14.refs_0_), channel_id=1, source_target_pairs={{0,1},{1,0},{2,3},{3,2},{4,5},{5,4},{6,7},{7,6},{8,9},{9,8},{10,11... | collective-permute-start | bytes 393224 | tf_op jit(solution)/shard_map/ppermute | solution.py:239
  13.2 6.1 %collective-permute-start.4 = (bf16[32,2048]{1,0:T(8,128)(2,1)S(1)}, bf16[32,2048]{1,0:T(8,128)(2,1)S(1)}, u32[]{:S(2)}, u32[]{:S(2)}) collective-permute-start(bf16[32,2048]{1,0:T(8,128)(2,1)S(1)} %collective-permute-done.2.refs_4_), channel_id=1, source_target_pairs={{0,1},{1,0},{2,3},{3,2},{4,5},{5,4},{6,7},{7,6},{8,9},{9,8},{10,11... | collective-permute-start | bytes 393224 | tf_op jit(solution)/shard_map/ppermute | solution.py:239
  14.8 6.3 %collective-permute-start.5 = (bf16[32,2048]{1,0:T(8,128)(2,1)S(1)}, bf16[32,2048]{1,0:T(8,128)(2,1)S(1)}, u32[]{:S(2)}, u32[]{:S(2)}) collective-permute-start(bf16[32,2048]{1,0:T(8,128)(2,1)S(1)} %collective-permute-done.2.refs_4_), channel_id=1, source_target_pairs={{0,2},{1,3},{2,0},{3,1},{4,6},{5,7},{6,4},{7,5},{8,10},{9,11},{10,... | collective-permute-start | bytes 393224 | tf_op jit(solution)/shard_map/ppermute | solution.py:239
  16.2 5.0 %collective-permute-start.3 = (bf16[32,2048]{1,0:T(8,128)(2,1)S(1)}, bf16[32,2048]{1,0:T(8,128)(2,1)S(1)}, u32[]{:S(2)}, u32[]{:S(2)}) collective-permute-start(bf16[32,2048]{1,0:T(8,128)(2,1)S(1)} %collective-permute-done.1.refs_2_), channel_id=1, source_target_pairs={{0,1},{1,0},{2,3},{3,2},{4,5},{5,4},{6,7},{7,6},{8,9},{9,8},{10,11... | collective-permute-start | bytes 393224 | tf_op jit(solution)/shard_map/ppermute | solution.py:239
  19.3 5.0 %collective-permute-start.6 = (bf16[32,2048]{1,0:T(8,128)(2,1)S(1)}, bf16[32,2048]{1,0:T(8,128)(2,1)S(1)}, u32[]{:S(2)}, u32[]{:S(2)}) collective-permute-start(bf16[32,2048]{1,0:T(8,128)(2,1)S(1)} %collective-permute-done.4.refs_5_), channel_id=1, source_target_pairs={{0,2},{1,3},{2,0},{3,1},{4,6},{5,7},{6,4},{7,5},{8,10},{9,11},{10,... | collective-permute-start | bytes 393224 | tf_op jit(solution)/shard_map/ppermute | solution.py:239
  34.6 4.5 %collective-permute-start.7 = (f32[4,128]{1,0:T(4,128)S(1)}, f32[4,128]{1,0:T(4,128)S(1)}, u32[]{:S(2)}, u32[]{:S(2)}) collective-permute-start(f32[4,128]{1,0:T(4,128)S(1)} %get-tuple-element.19), channel_id=1, source_target_pairs={{0,4},{1,5},{2,6},{3,7},{4,0},{5,1},{6,2},{7,3},{8,12},{9,13},{10,... | collective-permute-start | bytes 6152 | tf_op jit(solution)/shard_map/ppermute | solution.py:239
  39.3 3.6 %collective-permute-start.8 = (f32[4,64]{1,0:T(4,128)S(1)}, f32[4,64]{1,0:T(4,128)S(1)}, u32[]{:S(2)}, u32[]{:S(2)}) collective-permute-start(f32[4,64]{1,0:T(4,128)S(1)} %slice.117), channel_id=1, source_target_pairs={{0,2},{1,3},{2,0},{3,1},{4,6},{5,7},{6,4},{7,5},{8,10},{9,11},{10,... | collective-permute-start | bytes 3080 | tf_op jit(solution)/shard_map/ppermute | solution.py:239
  43.0 3.6 %collective-permute-start.9 = (f32[4,32]{1,0:T(4,128)S(1)}, f32[4,32]{1,0:T(4,128)S(1)}, u32[]{:S(2)}, u32[]{:S(2)}) collective-permute-start(f32[4,32]{1,0:T(4,128)S(1)} %slice.126), channel_id=1, source_target_pairs={{0,1},{1,0},{2,3},{3,2},{4,5},{5,4},{6,7},{7,6},{8,9},{9,8},{10,11... | collective-permute-start | bytes 1544 | tf_op jit(solution)/shard_map/ppermute | solution.py:239
